TPU v7x, 512 devices: a whole 4x4x16 slice. The times are simulated.
512 devices in a mesh: alpha: 32 (over y, x, core), beta: 16 (over z).
Axes of the slice: x: 4, y: 4, z: 16, core: 2. Of those that a mesh axis runs over, the one named last changes fastest.
Arguments:
- coeffs: bfloat16 [8192, 8192], P('alpha', 'beta'), may hold values from -6 to 6, as said below
- requests: int32 [32, 32, 16], P('alpha'), may hold values from 0 to 255, as said below
- repl_slot: int32 [32, 8192], P(None, 'alpha'), may hold values from 0 to 511, as said below
- repl_sign: int32 [32, 8192], P(None, 'alpha'), may hold values from -1 to 1
- pair_integrals: bfloat16 [32, 32], replicated, may hold values from -0.375 to 0.375
Outputs:
- sigma: float32 [8192, 8192], P('alpha', 'beta')
Inputs may be any that keep to these rules, and one draw needn't show every extreme that they name: coeffs equals its transpose. Each list of requests names distinct strings first and is padded with 0 after them; every list holds at least one string. repl_slot always names a filled entry of its string's own tile's lists.
All inputs are finite; a program needn't handle non-finite values.
Results may differ from a plain program's by a relative error of at most 0.0029.
Values may be sent and summed in bfloat16 or wider, within the bound.
No kernel may reach another device: no remote copies, remote signals or barrier semaphores. Data moves between devices by JAX's collectives and lax.ppermute only.
A program may use at most 128 MiB of HBM per device.

v0:
```python
import jax
import jax.numpy as jnp
from jax import lax
from jax.sharding import PartitionSpec as P


def local(coeffs, requests, repl_slot, repl_sign, pair_integrals):
    rows, cols = coeffs.shape
    peers = lax.axis_size("alpha")
    wanted = requests[0]
    cap = wanted.shape[1]
    width = peers * cap
    asked = lax.all_to_all(wanted, "alpha", split_axis=0, concat_axis=0, tiled=True)
    found = coeffs[asked]
    fetched = lax.all_to_all(found, "alpha", split_axis=0, concat_axis=0, tiled=True)
    fetched = fetched.reshape(width, cols)
    npairs = repl_slot.shape[0]
    blocks = npairs // 4
    slot_blocks = repl_slot.reshape(blocks, 4, rows)
    sign_blocks = repl_sign.reshape(blocks, 4, rows)
    entries = jnp.arange(width, dtype=jnp.int32)

    def one_hot(slot, sign):
        table = (slot[:, :, None] == entries[None, None, :]).astype(jnp.bfloat16)
        return table * sign.astype(jnp.bfloat16)[:, :, None]

    def replaced(pieces):
        table = one_hot(pieces[0], pieces[1])
        return jnp.einsum("pak,kb->pab", table, fetched, preferred_element_type=jnp.float32).astype(
            jnp.bfloat16
        )

    moved = lax.map(replaced, (slot_blocks, sign_blocks)).reshape(npairs, rows, cols)
    mixed = jnp.einsum(
        "qp,pab->qab", pair_integrals, moved, preferred_element_type=jnp.float32
    ).astype(jnp.bfloat16)
    mixed_blocks = mixed.reshape(blocks, 4, rows, cols)

    def spread(total, pieces):
        table = one_hot(pieces[0], pieces[1])
        return (
            total + jnp.einsum("pak,pab->kb", table, pieces[2], preferred_element_type=jnp.float32),
            None,
        )

    contrib, _ = lax.scan(
        spread, jnp.zeros((width, cols), jnp.float32), (slot_blocks, sign_blocks, mixed_blocks)
    )
    returned = lax.all_to_all(
        contrib.reshape(peers, cap, cols), "alpha", split_axis=0, concat_axis=0, tiled=True
    )
    owner_table = (asked.reshape(-1)[None, :] == jnp.arange(rows, dtype=jnp.int32)[:, None]).astype(
        jnp.float32
    )
    half_sigma = jnp.dot(
        owner_table,
        returned.reshape(width, cols),
        precision=lax.Precision.HIGHEST,
        preferred_element_type=jnp.float32,
    )
    groups = lax.axis_size("beta")
    ratio = peers // groups
    stripe = rows // groups
    strips = lax.all_to_all(half_sigma, "beta", split_axis=0, concat_axis=1, tiled=True)
    columns_in = lax.all_to_all(strips, "alpha", split_axis=1, concat_axis=0, tiled=True)
    grouped = lax.all_to_all(columns_in, "beta", split_axis=0, concat_axis=0, tiled=True)
    turned = jnp.transpose(grouped.reshape(groups, ratio, stripe, rows), (3, 1, 0, 2)).reshape(
        rows, cols
    )
    return half_sigma + turned


def solution(mesh):
    in_specs = (P("alpha", "beta"), P("alpha", None, None), P(None, "alpha"), P(None, "alpha"), P())
    out_specs = P("alpha", "beta")
    return jax.shard_map(local, mesh=mesh, in_specs=in_specs, out_specs=out_specs, check_vma=False)
```

profile of v0, /device:TPU:34, one launch (start us, length us, event | category | flops | bytes accessed | tf_op | source)
XLA Modules:
  0.0 216.1 jit_solution(10230572800164031177)
XLA Ops:
  0.8 13.6 %all_to_all.63 = s32[32,1,16]{2,1,0:T(1,128)S(1)} all-to-all(s32[32,1,16]{2,1,0:T(1,128)S(1)} %bitcast.69), channel_id=1, replica_groups=mesh['alpha'=32,'beta'=16] {'alpha'}, dimensions={0} | all-to-all | bytes 4096 | tf_op jit(solution)/shard_map/all_to_all | solution.py:13
  14.5 2.6 %gather_fusion = bf16[512,512]{1,0:T(8,128)(2,1)} fusion(bf16[256,512]{1,0:T(8,128)(2,1)S(1)} %copy-done, s32[1024]{0:T(1024)S(1)} %pad_clamp_fusion), kind=kCustom, calls=%fused_computation | custom fusion | bytes 1050624 | tf_op jit(solution)/shard_map/gather | solution.py:14
  17.1 5.0 %all-to-all-start.1 = ((bf16[32,16,512]{2,1,0:T(8,128)(2,1)}), bf16[32,16,512]{2,1,0:T(8,128)(2,1)S(1)}, u32[]{:S(2)}, u32[]{:S(2)}) async-start(bf16[32,16,512]{2,1,0:T(8,128)(2,1)} %bitcast.2), calls=%async_computation.1 | async-start | bytes 1048576 | tf_op jit(solution)/shard_map/all_to_all | solution.py:15
  23.7 9.0 %all-to-all-done.1 = bf16[32,16,512]{2,1,0:T(8,128)(2,1)S(1)} async-done(((bf16[32,16,512]{2,1,0:T(8,128)(2,1)}), bf16[32,16,512]{2,1,0:T(8,128)(2,1)S(1)}, u32[]{:S(2)}, u32[]{:S(2)}) %all-to-all-start.1) | async-done | bytes 524320 | tf_op jit(solution)/shard_map/all_to_all | solution.py:15
  32.7 14.1 %while.22 = (s32[]{:T(128)}, bf16[8,4,256,512]{3,2,1,0:T(8,128)(2,1)}, s32[8,4,256]{2,1,0:T(4,128)S(1)}, s32[8,4,256]{2,1,0:T(4,128)S(1)}, bf16[512,512]{1,0:T(8,128)(2,1)S(1)}, /*index=5*/s32[]{:T(128)}) while((s32[]{:T(128)}, bf16[8,4,256,512]{3,2,1,0:T(8,128)(2,1)}, s32[8,4,256]{2,1,0:T(4,128)S(1)}, s32[8,4,256]{2,1,0:T(4,128)S(1)}, ...), condition=%wide.region_1.2_spmd.clone, body=%wide.region_0.1_spmd.clone.sunk | while | flops 538444800 | bytes 1593929 | solution.py:33
  34.4 1.8 fusion.41
  41.5 1.8 fusion.41
  45.1 1.8 fusion.41
  46.8 13.1 %convert_bitcast_fusion = bf16[32,256,512]{2,0,1:T(8,128)(2,1)} fusion(bf16[32,256,512]{2,1,0:T(8,128)(2,1)} %bitcast.60, bf16[32,32]{1,0:T(8,128)(2,1)S(1)} %copy-done.1), kind=kOutput, calls=%fused_computation.32 | convolution fusion | flops 272629760 | bytes 16779264 | tf_op jit(solution)/shard_map/qp,pab->qab/dot_general | solution.py:34
  59.9 11.4 %copy.23 = bf16[32,256,512]{2,1,0:T(8,128)(2,1)} copy(bf16[32,256,512]{2,0,1:T(8,128)(2,1)} %convert_bitcast_fusion) | data formatting | bytes 16777216
  71.2 25.5 %while.23 = (s32[]{:T(128)}, f32[512,512]{1,0:T(8,128)}, s32[8,4,256]{2,1,0:T(4,128)S(1)}, s32[8,4,256]{2,1,0:T(4,128)S(1)}, bf16[8,4,256,512]{3,2,1,0:T(8,128)(2,1)}, /*index=5*/s32[]{:T(128)}, s32[]{:T(128)}) while((s32[]{:T(128)}, f32[512,512]{1,0:T(8,128)}, s32[8,4,256]{2,1,0:T(4,128)S(1)}, s32[8,4,256]{2,1,0:T(4,128)S(1)}, ...), condition=%wide.region_3.4_spmd.clone, body=%wide.region_2.3_spmd.clone.sunk | while | flops 538444800 | bytes 3166811 | solution.py:46
  71.2 2.9 %fusion.44 = f32[512,512]{1,0:T(8,128)} fusion(f32[512,512]{1,0:T(8,128)} %get-tuple-element.238, bf16[8,4,256,512]{3,2,1,0:T(8,128)(2,1)} %get-tuple-element.248, s32[]{:T(128)} %get-tuple-element.237, s32[4,256]{1,0:T(4,128)S(1)} %get-tuple-element.210, bf16[4,256]{1,0:T(4,128)(2,1)S(1)} %get-tuple-element.211, pred[]{:T(512)S(6)} %compare.3), kind=kOutput, calls=%fused_computation.19.clone.1 | convolution fusion | flops 538443776 | bytes 3152385 | tf_op jit(solution)/shard_map/while/body/eval_jaxpr/pak,pab->kb/dot_general | solution.py:42
  74.2 3.2 %fusion.44 = f32[512,512]{1,0:T(8,128)} fusion(f32[512,512]{1,0:T(8,128)} %get-tuple-element.238, bf16[8,4,256,512]{3,2,1,0:T(8,128)(2,1)} %get-tuple-element.248, s32[]{:T(128)} %get-tuple-element.237, s32[4,256]{1,0:T(4,128)S(1)} %get-tuple-element.210, bf16[4,256]{1,0:T(4,128)(2,1)S(1)} %get-tuple-element.211, pred[]{:T(512)S(6)} %compare.3), kind=kOutput, calls=%fused_computation.19.clone.1 | convolution fusion | flops 538443776 | bytes 3152385 | tf_op jit(solution)/shard_map/while/body/eval_jaxpr/pak,pab->kb/dot_general | solution.py:42
  77.4 3.2 %fusion.44 = f32[512,512]{1,0:T(8,128)} fusion(f32[512,512]{1,0:T(8,128)} %get-tuple-element.238, bf16[8,4,256,512]{3,2,1,0:T(8,128)(2,1)} %get-tuple-element.248, s32[]{:T(128)} %get-tuple-element.237, s32[4,256]{1,0:T(4,128)S(1)} %get-tuple-element.210, bf16[4,256]{1,0:T(4,128)(2,1)S(1)} %get-tuple-element.211, pred[]{:T(512)S(6)} %compare.3), kind=kOutput, calls=%fused_computation.19.clone.1 | convolution fusion | flops 538443776 | bytes 3152385 | tf_op jit(solution)/shard_map/while/body/eval_jaxpr/pak,pab->kb/dot_general | solution.py:42
  80.6 3.2 %fusion.44 = f32[512,512]{1,0:T(8,128)} fusion(f32[512,512]{1,0:T(8,128)} %get-tuple-element.238, bf16[8,4,256,512]{3,2,1,0:T(8,128)(2,1)} %get-tuple-element.248, s32[]{:T(128)} %get-tuple-element.237, s32[4,256]{1,0:T(4,128)S(1)} %get-tuple-element.210, bf16[4,256]{1,0:T(4,128)(2,1)S(1)} %get-tuple-element.211, pred[]{:T(512)S(6)} %compare.3), kind=kOutput, calls=%fused_computation.19.clone.1 | convolution fusion | flops 538443776 | bytes 3152385 | tf_op jit(solution)/shard_map/while/body/eval_jaxpr/pak,pab->kb/dot_general | solution.py:42
  83.8 3.2 %fusion.44 = f32[512,512]{1,0:T(8,128)} fusion(f32[512,512]{1,0:T(8,128)} %get-tuple-element.238, bf16[8,4,256,512]{3,2,1,0:T(8,128)(2,1)} %get-tuple-element.248, s32[]{:T(128)} %get-tuple-element.237, s32[4,256]{1,0:T(4,128)S(1)} %get-tuple-element.210, bf16[4,256]{1,0:T(4,128)(2,1)S(1)} %get-tuple-element.211, pred[]{:T(512)S(6)} %compare.3), kind=kOutput, calls=%fused_computation.19.clone.1 | convolution fusion | flops 538443776 | bytes 3152385 | tf_op jit(solution)/shard_map/while/body/eval_jaxpr/pak,pab->kb/dot_general | solution.py:42
  87.1 3.2 %fusion.44 = f32[512,512]{1,0:T(8,128)} fusion(f32[512,512]{1,0:T(8,128)} %get-tuple-element.238, bf16[8,4,256,512]{3,2,1,0:T(8,128)(2,1)} %get-tuple-element.248, s32[]{:T(128)} %get-tuple-element.237, s32[4,256]{1,0:T(4,128)S(1)} %get-tuple-element.210, bf16[4,256]{1,0:T(4,128)(2,1)S(1)} %get-tuple-element.211, pred[]{:T(512)S(6)} %compare.3), kind=kOutput, calls=%fused_computation.19.clone.1 | convolution fusion | flops 538443776 | bytes 3152385 | tf_op jit(solution)/shard_map/while/body/eval_jaxpr/pak,pab->kb/dot_general | solution.py:42
  90.3 3.2 %fusion.44 = f32[512,512]{1,0:T(8,128)} fusion(f32[512,512]{1,0:T(8,128)} %get-tuple-element.238, bf16[8,4,256,512]{3,2,1,0:T(8,128)(2,1)} %get-tuple-element.248, s32[]{:T(128)} %get-tuple-element.237, s32[4,256]{1,0:T(4,128)S(1)} %get-tuple-element.210, bf16[4,256]{1,0:T(4,128)(2,1)S(1)} %get-tuple-element.211, pred[]{:T(512)S(6)} %compare.3), kind=kOutput, calls=%fused_computation.19.clone.1 | convolution fusion | flops 538443776 | bytes 3152385 | tf_op jit(solution)/shard_map/while/body/eval_jaxpr/pak,pab->kb/dot_general | solution.py:42
  93.5 3.2 %fusion.44 = f32[512,512]{1,0:T(8,128)} fusion(f32[512,512]{1,0:T(8,128)} %get-tuple-element.238, bf16[8,4,256,512]{3,2,1,0:T(8,128)(2,1)} %get-tuple-element.248, s32[]{:T(128)} %get-tuple-element.237, s32[4,256]{1,0:T(4,128)S(1)} %get-tuple-element.210, bf16[4,256]{1,0:T(4,128)(2,1)S(1)} %get-tuple-element.211, pred[]{:T(512)S(6)} %compare.3), kind=kOutput, calls=%fused_computation.19.clone.1 | convolution fusion | flops 538443776 | bytes 3152385 | tf_op jit(solution)/shard_map/while/body/eval_jaxpr/pak,pab->kb/dot_general | solution.py:42
  96.7 5.1 %all-to-all-start.2 = ((f32[32,16,512]{2,1,0:T(8,128)}), f32[32,16,512]{2,1,0:T(8,128)S(1)}, u32[]{:S(2)}, u32[]{:S(2)}) async-start(f32[32,16,512]{2,1,0:T(8,128)} %bitcast.8), calls=%async_computation.2 | async-start | bytes 2097152 | tf_op jit(solution)/shard_map/all_to_all | solution.py:49
  103.1 14.9 %all-to-all-done.2 = f32[32,16,512]{2,1,0:T(8,128)S(1)} async-done(((f32[32,16,512]{2,1,0:T(8,128)}), f32[32,16,512]{2,1,0:T(8,128)S(1)}, u32[]{:S(2)}, u32[]{:S(2)}) %all-to-all-start.2) | async-done | bytes 1048608 | tf_op jit(solution)/shard_map/all_to_all | solution.py:49
  118.7 44.5 %all_to_all.64 = f32[16,16,512]{2,1,0:T(8,128)S(1)} all-to-all(f32[16,16,512]{2,1,0:T(8,128)S(1)} %bitcast.61), channel_id=1, replica_groups=mesh['alpha'=32,'beta'=16] {'beta'}, dimensions={0} | all-to-all | bytes 1048576 | tf_op jit(solution)/shard_map/all_to_all | solution.py:64
  164.0 14.3 %all_to_all.65 = f32[16,32,256]{2,0,1:T(8,128)S(1)} all-to-all(f32[16,32,256]{2,0,1:T(8,128)S(1)} %copy.20), channel_id=1, replica_groups=mesh['alpha'=32,'beta'=16] {'alpha'}, dimensions={1} | all-to-all | bytes 1048576 | tf_op jit(solution)/shard_map/all_to_all | solution.py:65
  178.3 36.7 %all_to_all.66 = f32[16,32,256]{2,1,0:T(8,128)S(1)} all-to-all(f32[16,32,256]{2,1,0:T(8,128)S(1)} %bitcast.63), channel_id=1, replica_groups=mesh['alpha'=32,'beta'=16] {'beta'}, dimensions={0} | all-to-all | bytes 1048576 | tf_op jit(solution)/shard_map/all_to_all | solution.py:66
  (43 shorter events, 15.0 us)
Async XLA Ops:
  0.0 14.5 %copy-start = (bf16[256,512]{1,0:T(8,128)(2,1)S(1)}, bf16[256,512]{1,0:T(8,128)(2,1)}, u32[]{:S(2)}) copy-start(bf16[256,512]{1,0:T(8,128)(2,1)} %param.9) | copy-start | bytes 786436
  17.1 15.6 %all-to-all-start.1 = ((bf16[32,16,512]{2,1,0:T(8,128)(2,1)}), bf16[32,16,512]{2,1,0:T(8,128)(2,1)S(1)}, u32[]{:S(2)}, u32[]{:S(2)}) async-start(bf16[32,16,512]{2,1,0:T(8,128)(2,1)} %bitcast.2), calls=%async_computation.1 | async-start | bytes 1048576 | tf_op jit(solution)/shard_map/all_to_all | solution.py:15
  32.7 14.1 %copy-start.1 = (bf16[32,32]{1,0:T(8,128)(2,1)S(1)}, bf16[32,32]{1,0:T(8,128)(2,1)}, u32[]{:S(2)}) copy-start(bf16[32,32]{1,0:T(8,128)(2,1)} %param.13) | copy-start | bytes 6148
  96.7 21.3 %all-to-all-start.2 = ((f32[32,16,512]{2,1,0:T(8,128)}), f32[32,16,512]{2,1,0:T(8,128)S(1)}, u32[]{:S(2)}, u32[]{:S(2)}) async-start(f32[32,16,512]{2,1,0:T(8,128)} %bitcast.8), calls=%async_computation.2 | async-start | bytes 2097152 | tf_op jit(solution)/shard_map/all_to_all | solution.py:49
where the time goes:
time: 217 us; the launch traced here: 216 us
  blocking collectives  109 us (50%)
  matrix products  53.3 us (25%)
  waiting for transfers between devices  24 us (11%)
  local copies, waits for them, and re-layouts  17.9 us (8%)
  starting transfers between devices  10.1 us (5%)
    all_to_all x1, blocking collectives, local(): lax.all_to_all(half_sigma, 'beta', split_axis=0, concat_axis=1, tiled=True)  44.5 us
    all_to_all x1, blocking collectives, local(): lax.all_to_all(columns_in, 'beta', split_axis=0, concat_axis=0, tiled=True)  36.7 us
    dot_general x8, matrix products, spread(): jnp.einsum('pak,pab->kb', table, pieces[2], preferred_element_type=jnp.fl...  25.4 us
    all_to_all x1, waiting for transfers between devices, local(): lax.all_to_all(contrib.reshape(peers, cap, cols), 'alpha', split_axis=0,...  14.9 us
    all_to_all x1, blocking collectives, local(): lax.all_to_all(strips, 'alpha', split_axis=1, concat_axis=0, tiled=True)  14.3 us
    dot_general x8, matrix products, replaced(): jnp.einsum('pak,kb->pab', table, fetched, preferred_element_type=jnp.floa...  14.1 us
    all_to_all x1, blocking collectives, local(): lax.all_to_all(wanted, 'alpha', split_axis=0, concat_axis=0, tiled=True)  13.6 us
    dot_general x1, matrix products, local(): jnp.einsum('qp,pab->qab', pair_integrals, moved, preferred_element_type=j...  13.1 us
  transfers between devices with their start and end apart: 2, of which 2 were waited for; matrix products, arithmetic and copies ran while one was open for 1% of the time, Pallas kernels for 0%

commit v1 on v0

v1 whole, which is shorter than its diff:
```python
import jax
import jax.numpy as jnp
from jax import lax
from jax.experimental import pallas as pl
from jax.experimental.pallas import tpu as pltpu
from jax.sharding import PartitionSpec as P

F32 = jnp.float32
BF16 = jnp.bfloat16
VMEM = pltpu.VMEM


def flat_row(table, columns):
    n, m = table.shape
    width = n * m
    lane = lax.broadcasted_iota(jnp.int32, (m, width), 1)
    pick = (lane % m == lax.broadcasted_iota(jnp.int32, (m, width), 0)).astype(BF16)
    wide = jnp.dot(table.astype(F32).astype(BF16), pick, preferred_element_type=F32)
    lane = lax.broadcasted_iota(jnp.int32, (n, width), 1)
    mine = lane // m == lax.broadcasted_iota(jnp.int32, (n, width), 0)
    return jnp.sum(jnp.where(mine, wide, 0.0), axis=0, keepdims=True)


def one_hot(row, count):
    width = row.shape[1]
    lines = lax.broadcasted_iota(jnp.int32, (count, width), 0).astype(F32)
    return (lines == row).astype(F32).astype(BF16)


def coupling_kernel(slot_ref, sign_ref, kron_ref, high_ref, low_ref, total_ref):
    chunks, lanes = slot_ref.shape
    width = total_ref.shape[0]
    side = kron_ref.shape[0]
    line = lax.broadcasted_iota(jnp.int32, (16, lanes), 0).astype(F32).astype(BF16)
    total_ref[...] = jnp.zeros_like(total_ref)

    def step(c, carry):
        slots = (slot_ref[pl.ds(c, 1), :] - width // 2).astype(F32)
        signs = sign_ref[pl.ds(c, 1), :].astype(F32)
        slots = jnp.broadcast_to(slots, (16, lanes)).astype(BF16)
        signs = jnp.broadcast_to(signs, (16, lanes)).astype(BF16)
        zero = jnp.zeros((16, lanes), BF16)
        rows = []
        for k in range(width // 16):
            base = jnp.asarray(16 * k - width // 2, BF16)
            rows.append(jnp.where(slots == line + base, signs, zero))
        table = jnp.concatenate(rows, axis=0)
        mixed = [
            jnp.dot(table[:, n : n + side], kron_ref[...], preferred_element_type=F32).astype(BF16)
            for n in range(0, lanes, side)
        ]
        mixed = jnp.concatenate(mixed, axis=1)
        total_ref[...] += lax.dot_general(
            table, mixed, (((1,), (1,)), ((), ())), preferred_element_type=F32
        )
        return carry

    lax.fori_loop(0, chunks, step, 0)
    high = total_ref[...].astype(BF16)
    high_ref[...] = high
    low_ref[...] = (total_ref[...] - high.astype(F32)).astype(BF16)


def gather_kernel(asked_ref, coeffs_ref, found_ref):
    rows = coeffs_ref.shape[0]
    table = one_hot(flat_row(asked_ref[...], rows), rows)
    found = lax.dot_general(
        table, coeffs_ref[...], (((0,), (0,)), ((), ())), preferred_element_type=F32
    )
    found_ref[...] = found.astype(BF16)


def contributions_kernel(plane_ref, high_ref, low_ref, fetched_ref, extra_ref, own_ref):
    sites, two_cap, half = extra_ref.shape
    chips = sites // 2
    fetched = fetched_ref[...]
    contrib = jnp.dot(high_ref[...], fetched, preferred_element_type=F32)
    contrib += jnp.dot(low_ref[...], fetched, preferred_element_type=F32)
    own_ref[...] = contrib.astype(BF16)
    plane = plane_ref[0]
    for j in range(chips):
        for h in range(2):
            chip = lax.rem(j + 2 * chips - plane - h * (chips // 2), chips)
            start = pl.multiple_of(chip * two_cap, two_cap)
            extra_ref[2 * j + h] = own_ref[pl.ds(start, two_cap), h * half : (h + 1) * half]


def turned_kernel(cap, asked_ref, extra_ref, turned_ref):
    rows, cols = turned_ref.shape
    asked = flat_row(asked_ref[...], rows)
    width = asked.shape[1]
    lane = lax.broadcasted_iota(jnp.int32, (1, width), 1)
    core = (lane // cap) % 2
    table = one_hot(asked + (core * rows).astype(F32), cols)
    summed = jnp.dot(table, extra_ref[...], preferred_element_type=F32)
    turned_ref[...] = summed.T.astype(BF16)


def own_kernel(asked_ref, returned_ref, half_ref):
    rows = half_ref.shape[0]
    table = one_hot(flat_row(asked_ref[...], rows), rows)
    half_ref[...] = jnp.dot(table, returned_ref[...], preferred_element_type=F32)


def call(kernel, outs, operands, flops, moved, scratch=(), scalars=0):
    in_specs = [pl.BlockSpec(memory_space=pltpu.SMEM)] * scalars
    in_specs += [pl.BlockSpec(memory_space=VMEM)] * (len(operands) - scalars)
    many = isinstance(outs, (list, tuple))
    return pl.pallas_call(
        kernel,
        out_shape=outs,
        in_specs=in_specs,
        out_specs=[pl.BlockSpec(memory_space=VMEM)] * len(outs) if many else pl.BlockSpec(memory_space=VMEM),
        scratch_shapes=list(scratch),
        compiler_params=pltpu.CompilerParams(vmem_limit_bytes=40 * 2**20),
        cost_estimate=pl.CostEstimate(flops=flops, bytes_accessed=moved, transcendentals=0),
    )(*operands)


def local(coeffs, requests, repl_slot, repl_sign, pair_integrals):
    rows, cols = coeffs.shape
    peers = lax.axis_size("alpha")
    chips = lax.axis_size("beta")
    plane = lax.axis_index("beta").astype(jnp.int32)
    wanted = requests[0]
    cap = wanted.shape[1]
    width = peers * cap
    pairs = repl_slot.shape[0]

    by_chip = wanted.reshape(chips, 2 * cap)
    twice = jnp.concatenate([by_chip, by_chip], axis=0)
    shifted = [
        lax.dynamic_slice_in_dim(twice, (2 * chips - plane - h * (chips // 2)) % chips, chips, 0)
        for h in range(2)
    ]
    shifted = jnp.stack(shifted, axis=1).reshape(peers, 2 * cap)
    asked = lax.all_to_all(
        jnp.concatenate([wanted, shifted], axis=1), "alpha", split_axis=0, concat_axis=0, tiled=True
    )
    asked_own, asked_site = asked[:, :cap], asked[:, cap:]

    lanes = 1024 if (rows * pairs) % 1024 == 0 else rows * pairs
    group = 256 // pairs
    slot_rows = repl_slot.T.reshape(-1, lanes)
    sign_rows = repl_sign.T.reshape(-1, lanes)
    kron = jnp.kron(jnp.eye(group, dtype=BF16), pair_integrals.T)
    square = jax.ShapeDtypeStruct((width, width), BF16)
    high, low = call(
        coupling_kernel,
        [square, square],
        (slot_rows, sign_rows, kron),
        2 * rows * pairs * width * (width + 256),
        4 * width * width,
        scratch=[VMEM((width, width), F32)],
    )

    found = call(
        gather_kernel,
        jax.ShapeDtypeStruct((width, cols), BF16),
        (asked_own, coeffs),
        2 * width * rows * cols,
        2 * (width + rows) * cols,
    )
    fetched = lax.all_to_all(
        found.reshape(peers, cap, cols), "alpha", split_axis=0, concat_axis=0, tiled=True
    ).reshape(width, cols)

    extra, own = call(
        contributions_kernel,
        [jax.ShapeDtypeStruct((peers, 2 * cap, cols // 2), BF16), jax.ShapeDtypeStruct((width, cols), BF16)],
        (plane.reshape(1), high, low, fetched),
        4 * width * width * cols,
        4 * width * width + 6 * width * cols,
        scalars=1,
    )
    extra = lax.all_to_all(extra, "alpha", split_axis=0, concat_axis=0, tiled=True)

    turned = call(
        lambda *refs: turned_kernel(cap, *refs),
        jax.ShapeDtypeStruct((rows, cols), BF16),
        (asked_site, extra.reshape(2 * width, cols // 2)),
        2 * cols * width * cols,
        2 * (width + rows) * cols,
    )
    own, turned = lax.optimization_barrier((own, turned))
    places = []
    for j in range(chips):
        for h in range(2):
            for z in range(chips):
                l = (j - z - h * (chips // 2)) % chips
                places.append(((2 * j + h) * chips + z, (2 * z + h) * chips + l))
    turned = lax.ppermute(turned, ("alpha", "beta"), places)
    returned = lax.all_to_all(
        own.reshape(peers, cap, cols), "alpha", split_axis=0, concat_axis=0, tiled=True
    ).reshape(width, cols)
    half_sigma = call(
        own_kernel,
        jax.ShapeDtypeStruct((rows, cols), F32),
        (asked_own, returned),
        2 * width * rows * cols,
        2 * width * cols + 4 * rows * cols,
    )
    return half_sigma + turned.astype(F32)


def solution(mesh):
    in_specs = (P("alpha", "beta"), P("alpha", None, None), P(None, "alpha"), P(None, "alpha"), P())
    out_specs = P("alpha", "beta")
    return jax.shard_map(local, mesh=mesh, in_specs=in_specs, out_specs=out_specs, check_vma=False)
```

time: 217 us -> 87.2 us (0.40)
  the two profiles are of different devices: /device:TPU:34 before, /device:TPU:320 now
where the time goes in v1:
time: 87.2 us; the launch traced here: 86.6 us
  waiting for transfers between devices  43.2 us (50%)
  starting transfers between devices  26.7 us (31%)
  Pallas kernels  12.1 us (14%)
  local copies, waits for them, and re-layouts  2.72 us (3%)
  other arithmetic  1.68 us (2%)
    ppermute x1, waiting for transfers between devices, local(): turned = lax.ppermute(turned, ('alpha', 'beta'), places)  18.4 us
    pallas_call x5, Pallas kernels, call(): pl.pallas_call(kernel, out_shape=outs, in_specs=in_specs, out_specs=[pl.B...  12.1 us
    all_to_all x1, waiting for transfers between devices, local(): lax.all_to_all(extra, 'alpha', split_axis=0, concat_axis=0, tiled=True)  11.7 us
    ppermute x1, starting transfers between devices, local(): turned = lax.ppermute(turned, ('alpha', 'beta'), places)  7.6 us
    all_to_all x1, starting transfers between devices, local(): lax.all_to_all(jnp.concatenate([wanted, shifted], axis=1), 'alpha', split...  7.45 us
    all_to_all x1, waiting for transfers between devices, local(): lax.all_to_all(jnp.concatenate([wanted, shifted], axis=1), 'alpha', split...  5.33 us
    all_to_all x1, waiting for transfers between devices, local(): lax.all_to_all(own.reshape(peers, cap, cols), 'alpha', split_axis=0, conc...  4.11 us
    all_to_all x1, starting transfers between devices, local(): lax.all_to_all(own.reshape(peers, cap, cols), 'alpha', split_axis=0, conc...  3.9 us
  transfers between devices with their start and end apart: 5, of which 5 were waited for; matrix products, arithmetic and copies ran while one was open for 1% of the time, Pallas kernels for 10%

profile of v1, /device:TPU:320, one launch (start us, length us, event | category | flops | bytes accessed | tf_op | source)
XLA Modules:
  0.0 86.6 jit_solution(5253367081670247099)
XLA Ops:
  0.0 0.7 copy-done.3
  0.9 0.7 pad_add_fusion.1
  1.6 7.5 %all-to-all-start = ((s32[32,1,48]{2,1,0:T(1,128)}), s32[32,1,48]{2,1,0:T(1,128)S(1)}, u32[]{:S(2)}, u32[]{:S(2)}) async-start(s32[32,1,48]{2,1,0:T(1,128)} %bitcast.4), calls=%async_computation | async-start | bytes 32768 | tf_op jit(solution)/shard_map/all_to_all | solution.py:137
  9.1 0.1 broadcast_multiply_fusion
  9.3 0.4 mul.27.kron_ref
  9.6 0.4 copy-done.1
  10.1 0.1 reshape.45.slot_ref
  10.2 0.5 copy-done.2
  10.9 0.1 reshape.46.sign_ref
  11.0 5.3 %all-to-all-done = s32[32,1,48]{2,1,0:T(1,128)S(1)} async-done(((s32[32,1,48]{2,1,0:T(1,128)}), s32[32,1,48]{2,1,0:T(1,128)S(1)}, u32[]{:S(2)}, u32[]{:S(2)}) %all-to-all-start) | async-done | bytes 6176 | tf_op jit(solution)/shard_map/all_to_all | solution.py:137
  16.3 1.2 %shard_map.56 = bf16[512,512]{1,0:T(8,128)(2,1)} custom-call(s32[32,16]{1,0:T(8,128)S(1)} %bitcast.21, bf16[256,512]{1,0:T(8,128)(2,1)S(1)} %copy-done), custom_call_target="tpu_custom_call" | custom-call | flops 134217728 | bytes 786432 | tf_op jit(solution)/shard_map/pallas_call | solution.py:109
  17.6 3.9 %all-to-all-start.1 = ((bf16[32,16,512]{2,1,0:T(8,128)(2,1)}), bf16[32,16,512]{2,1,0:T(8,128)(2,1)S(1)}, u32[]{:S(2)}, u32[]{:S(2)}) async-start(bf16[32,16,512]{2,1,0:T(8,128)(2,1)} %bitcast.10), calls=%async_computation.1 | async-start | bytes 1048576 | tf_op jit(solution)/shard_map/all_to_all | solution.py:164
  21.5 8.1 %shard_map.55 = (bf16[512,512]{1,0:T(8,128)(2,1)S(1)}, bf16[512,512]{1,0:T(8,128)(2,1)S(1)}) custom-call(s32[8,1024]{1,0:T(8,128)S(1)} %reshape.45.slot_ref, s32[8,1024]{1,0:T(8,128)S(1)} %reshape.46.sign_ref, bf16[256,256]{1,0:T(8,128)(2,1)S(1)} %mul.27.kron_ref), custom_call_target="tpu_custom_call" | custom-call | flops 6442450944 | bytes 1048576 | tf_op jit(solution)/shard_map/pallas_call | solution.py:109
  29.6 3.7 %all-to-all-done.1 = bf16[32,16,512]{2,1,0:T(8,128)(2,1)S(1)} async-done(((bf16[32,16,512]{2,1,0:T(8,128)(2,1)}), bf16[32,16,512]{2,1,0:T(8,128)(2,1)S(1)}, u32[]{:S(2)}, u32[]{:S(2)}) %all-to-all-start.1) | async-done | bytes 524320 | tf_op jit(solution)/shard_map/all_to_all | solution.py:164
  33.2 1.7 %shard_map.57 = (bf16[32,32,256]{2,1,0:T(8,128)(2,1)}, bf16[512,512]{1,0:T(8,128)(2,1)}) custom-call(s32[1]{0:T(128)} %bitcast.6.plane_ref, bf16[512,512]{1,0:T(8,128)(2,1)S(1)} %get-tuple-element.11.high_ref, bf16[512,512]{1,0:T(8,128)(2,1)S(1)} %get-tuple-element.12.low_ref, bf16[512,512]{1,0:T(8,128)(2,1)S(1)} %bitcast.19), custom_call_target="tpu_custom_call" | custom-call | flops 536870912 | bytes 2621440 | tf_op jit(solution)/shard_map/pallas_call | solution.py:109
  34.9 3.9 %all-to-all-start.2 = ((bf16[32,32,256]{2,1,0:T(8,128)(2,1)}), bf16[32,32,256]{2,1,0:T(8,128)(2,1)S(1)}, u32[]{:S(2)}, u32[]{:S(2)}) async-start(bf16[32,32,256]{2,1,0:T(8,128)(2,1)} %get-tuple-element.14), calls=%async_computation.2 | async-start | bytes 1048576 | tf_op jit(solution)/shard_map/all_to_all | solution.py:176
  38.9 11.7 %all-to-all-done.2 = bf16[32,32,256]{2,1,0:T(8,128)(2,1)S(1)} async-done(((bf16[32,32,256]{2,1,0:T(8,128)(2,1)}), bf16[32,32,256]{2,1,0:T(8,128)(2,1)S(1)}, u32[]{:S(2)}, u32[]{:S(2)}) %all-to-all-start.2) | async-done | bytes 524320 | tf_op jit(solution)/shard_map/all_to_all | solution.py:176
  50.6 0.6 shard_map.58
  51.2 3.9 %all-to-all-start.3 = ((bf16[32,16,512]{2,1,0:T(8,128)(2,1)}), bf16[32,16,512]{2,1,0:T(8,128)(2,1)S(1)}, u32[]{:S(2)}, u32[]{:S(2)}) async-start(bf16[32,16,512]{2,1,0:T(8,128)(2,1)} %bitcast.13), calls=%async_computation.3 | async-start | bytes 1048576 | tf_op jit(solution)/shard_map/all_to_all | solution.py:193
  55.1 7.6 %collective-permute-start = (bf16[256,512]{1,0:T(8,128)(2,1)S(1)}, bf16[256,512]{1,0:T(8,128)(2,1)S(1)}, u32[]{:S(2)}, u32[]{:S(2)}) collective-permute-start(bf16[256,512]{1,0:T(8,128)(2,1)S(1)} %shard_map.58), channel_id=1, source_target_pairs={{0,0},{1,47},{2,78},{3,109},{4,140},{5,171},{6,202},{7,233},{8,264... | collective-permute-start | bytes 786440 | tf_op jit(solution)/shard_map/ppermute | solution.py:192
  62.8 4.1 %all-to-all-done.3 = bf16[32,16,512]{2,1,0:T(8,128)(2,1)S(1)} async-done(((bf16[32,16,512]{2,1,0:T(8,128)(2,1)}), bf16[32,16,512]{2,1,0:T(8,128)(2,1)S(1)}, u32[]{:S(2)}, u32[]{:S(2)}) %all-to-all-start.3) | async-done | bytes 524320 | tf_op jit(solution)/shard_map/all_to_all | solution.py:193
  66.9 0.4 shard_map.59
  67.3 18.4 %collective-permute-done = bf16[256,512]{1,0:T(8,128)(2,1)S(1)} collective-permute-done((bf16[256,512]{1,0:T(8,128)(2,1)S(1)}, bf16[256,512]{1,0:T(8,128)(2,1)S(1)}, u32[]{:S(2)}, u32[]{:S(2)}) %collective-permute-start) | collective-permute-done | bytes 262176 | tf_op jit(solution)/shard_map/ppermute | solution.py:192
  85.7 0.9 %convert_add_fusion = f32[256,512]{1,0:T(8,128)} fusion(f32[256,512]{1,0:T(8,128)S(1)} %shard_map.59, bf16[256,512]{1,0:T(8,128)(2,1)S(1)} %collective-permute-done), kind=kLoop, calls=%fused_computation | loop fusion | flops 262144 | bytes 1310720 | tf_op jit(solution)/shard_map/add | solution.py:203
  (18 shorter events, 0.6 us)
Async XLA Ops:
  0.0 0.7 copy-start.3
  1.6 7.5 %copy-start.4 = (bf16[32,32]{1,0:T(8,128)(2,1)S(1)}, bf16[32,32]{1,0:T(8,128)(2,1)}, u32[]{:S(2)}) copy-start(bf16[32,32]{1,0:T(8,128)(2,1)} %param.9) | copy-start | bytes 6148
  1.6 14.7 %all-to-all-start = ((s32[32,1,48]{2,1,0:T(1,128)}), s32[32,1,48]{2,1,0:T(1,128)S(1)}, u32[]{:S(2)}, u32[]{:S(2)}) async-start(s32[32,1,48]{2,1,0:T(1,128)} %bitcast.4), calls=%async_computation | async-start | bytes 32768 | tf_op jit(solution)/shard_map/all_to_all | solution.py:137
  9.3 0.8 copy-start.1
  10.0 0.8 copy-start.2
  10.1 6.2 %copy-start = (bf16[256,512]{1,0:T(8,128)(2,1)S(1)}, bf16[256,512]{1,0:T(8,128)(2,1)}, u32[]{:S(2)}) copy-start(bf16[256,512]{1,0:T(8,128)(2,1)} %coeffs_ref.1) | copy-start | bytes 786436
  17.6 15.7 %all-to-all-start.1 = ((bf16[32,16,512]{2,1,0:T(8,128)(2,1)}), bf16[32,16,512]{2,1,0:T(8,128)(2,1)S(1)}, u32[]{:S(2)}, u32[]{:S(2)}) async-start(bf16[32,16,512]{2,1,0:T(8,128)(2,1)} %bitcast.10), calls=%async_computation.1 | async-start | bytes 1048576 | tf_op jit(solution)/shard_map/all_to_all | solution.py:164
  34.9 15.7 %all-to-all-start.2 = ((bf16[32,32,256]{2,1,0:T(8,128)(2,1)}), bf16[32,32,256]{2,1,0:T(8,128)(2,1)S(1)}, u32[]{:S(2)}, u32[]{:S(2)}) async-start(bf16[32,32,256]{2,1,0:T(8,128)(2,1)} %get-tuple-element.14), calls=%async_computation.2 | async-start | bytes 1048576 | tf_op jit(solution)/shard_map/all_to_all | solution.py:176
  51.2 15.6 %all-to-all-start.3 = ((bf16[32,16,512]{2,1,0:T(8,128)(2,1)}), bf16[32,16,512]{2,1,0:T(8,128)(2,1)S(1)}, u32[]{:S(2)}, u32[]{:S(2)}) async-start(bf16[32,16,512]{2,1,0:T(8,128)(2,1)} %bitcast.13), calls=%async_computation.3 | async-start | bytes 1048576 | tf_op jit(solution)/shard_map/all_to_all | solution.py:193
  55.1 30.6 %collective-permute-start = (bf16[256,512]{1,0:T(8,128)(2,1)S(1)}, bf16[256,512]{1,0:T(8,128)(2,1)S(1)}, u32[]{:S(2)}, u32[]{:S(2)}) collective-permute-start(bf16[256,512]{1,0:T(8,128)(2,1)S(1)} %shard_map.58), channel_id=1, source_target_pairs={{0,0},{1,47},{2,78},{3,109},{4,140},{5,171},{6,202},{7,233},{8,264... | collective-permute-start | bytes 786440 | tf_op jit(solution)/shard_map/ppermute | solution.py:192

commit v2 on v1

v2 whole, which is shorter than its diff:
```python
import jax
import jax.numpy as jnp
from jax import lax
from jax.experimental import pallas as pl
from jax.experimental.pallas import tpu as pltpu
from jax.sharding import PartitionSpec as P

F32 = jnp.float32
BF16 = jnp.bfloat16
VMEM = pltpu.VMEM


def flat_row(table, columns):
    n, m = table.shape
    width = n * m
    lane = lax.broadcasted_iota(jnp.int32, (m, width), 1)
    pick = (lane % m == lax.broadcasted_iota(jnp.int32, (m, width), 0)).astype(BF16)
    wide = jnp.dot(table.astype(F32).astype(BF16), pick, preferred_element_type=F32)
    lane = lax.broadcasted_iota(jnp.int32, (n, width), 1)
    mine = lane // m == lax.broadcasted_iota(jnp.int32, (n, width), 0)
    return jnp.sum(jnp.where(mine, wide, 0.0), axis=0, keepdims=True)


def one_hot(row, count):
    width = row.shape[1]
    lines = lax.broadcasted_iota(jnp.int32, (count, width), 0).astype(F32)
    return (lines == row).astype(F32).astype(BF16)


def ask_kernel(wanted_ref, ask_ref):
    cap, peers = wanted_ref.shape
    chips = peers // 2
    plane = lax.axis_index("beta")
    site = lax.broadcasted_iota(jnp.int32, (peers, peers), 0)
    tile = lax.broadcasted_iota(jnp.int32, (peers, peers), 1)
    chip = site // 2 - plane - (site % 2) * (chips // 2)
    chip = jnp.where(chip < 0, chip + chips, chip)
    chip = jnp.where(chip < 0, chip + chips, chip)
    wanted = wanted_ref[...].astype(F32).astype(BF16)
    for part, source in enumerate((site, 2 * chip, 2 * chip + 1)):
        pick = (tile == source).astype(F32).astype(BF16)
        lists = lax.dot_general(pick, wanted, (((1,), (1,)), ((), ())), preferred_element_type=F32)
        ask_ref[:, part * cap : (part + 1) * cap] = lists.astype(jnp.int32)


def coupling_kernel(slot_ref, sign_ref, kron_ref, high_ref, low_ref, total_ref):
    chunks, lanes = slot_ref.shape
    width = total_ref.shape[0]
    side = kron_ref.shape[0]
    line = lax.broadcasted_iota(jnp.int32, (16, lanes), 0).astype(F32).astype(BF16)
    total_ref[...] = jnp.zeros_like(total_ref)

    def step(c, carry):
        slots = (slot_ref[pl.ds(c, 1), :] - width // 2).astype(F32)
        signs = sign_ref[pl.ds(c, 1), :].astype(F32)
        slots = jnp.broadcast_to(slots, (16, lanes)).astype(BF16)
        signs = jnp.broadcast_to(signs, (16, lanes)).astype(BF16)
        zero = jnp.zeros((16, lanes), BF16)
        rows = []
        for k in range(width // 16):
            base = jnp.asarray(16 * k - width // 2, BF16)
            rows.append(jnp.where(slots == line + base, signs, zero))
        table = jnp.concatenate(rows, axis=0)
        mixed = [
            jnp.dot(table[:, n : n + side], kron_ref[...], preferred_element_type=F32).astype(BF16)
            for n in range(0, lanes, side)
        ]
        mixed = jnp.concatenate(mixed, axis=1)
        total_ref[...] += lax.dot_general(
            table, mixed, (((1,), (1,)), ((), ())), preferred_element_type=F32
        )
        return carry

    lax.fori_loop(0, chunks, step, 0)
    high = total_ref[...].astype(BF16)
    high_ref[...] = high
    low_ref[...] = (total_ref[...] - high.astype(F32)).astype(BF16)


def gather_kernel(asked_ref, coeffs_ref, found_ref):
    rows = coeffs_ref.shape[0]
    peers, cap = asked_ref.shape
    line = lax.broadcasted_iota(jnp.int32, (cap, cap), 0)
    same = (line == lax.broadcasted_iota(jnp.int32, (cap, cap), 1)).astype(F32).astype(BF16)
    asked = asked_ref[...].astype(F32).astype(BF16)
    asked = lax.dot_general(same, asked, (((1,), (1,)), ((), ())), preferred_element_type=F32)
    lane = lax.broadcasted_iota(jnp.int32, (cap, rows), 1).astype(F32)
    table = [(asked[:, t : t + 1] == lane).astype(F32).astype(BF16) for t in range(peers)]
    found = jnp.dot(jnp.concatenate(table, axis=0), coeffs_ref[...], preferred_element_type=F32)
    found_ref[...] = found.astype(BF16)


def contributions_kernel(high_ref, low_ref, fetched_ref, sites_ref, owners_ref):
    sites, two_cap, half = sites_ref.shape
    chips = sites // 2
    plane = lax.axis_index("beta")
    fetched = fetched_ref[...]
    contrib = jnp.dot(high_ref[...], fetched, preferred_element_type=F32)
    contrib += jnp.dot(low_ref[...], fetched, preferred_element_type=F32)
    owners_ref[...] = contrib.astype(BF16)
    for j in range(chips):
        for h in range(2):
            chip = lax.rem(j + 2 * chips - plane - h * (chips // 2), chips)
            start = pl.multiple_of(chip * two_cap, two_cap)
            sites_ref[2 * j + h] = owners_ref[pl.ds(start, two_cap), h * half : (h + 1) * half]


def site_kernel(cap, asked_ref, contrib_ref, sent_ref):
    cols, rows = sent_ref.shape
    asked = flat_row(asked_ref[...], rows)
    lane = lax.broadcasted_iota(jnp.int32, asked.shape, 1)
    core = (lane // cap) % 2
    table = one_hot(asked + (core * rows).astype(F32), cols)
    sent_ref[...] = jnp.dot(table, contrib_ref[...], preferred_element_type=F32).astype(BF16)


def turn_kernel(sent_ref, turned_ref):
    turned_ref[...] = sent_ref[...].astype(F32).T


def from_third(chips):
    source, place = lax.axis_index("alpha") // 2, lax.axis_index("beta")
    return jnp.logical_and(source < chips // 2, place < chips // 2)


def choose_kernel(first_ref, second_ref, turned_ref):
    chips = lax.axis_size("beta")
    from_first = lax.axis_index("alpha") // 2 < chips // 2

    @pl.when(from_first)
    def _():
        turned_ref[...] = first_ref[...]

    @pl.when(jnp.logical_not(from_first))
    def _():
        turned_ref[...] = second_ref[...].astype(F32).T


def own_kernel(asked_ref, contrib_ref, turned_ref, part_ref):
    rows = part_ref.shape[0]
    table = one_hot(flat_row(asked_ref[...], rows), rows)
    part_ref[...] = jnp.dot(table, contrib_ref[...], preferred_element_type=F32) + turned_ref[...]


def sigma_kernel(part_ref, third_ref, sigma_ref):
    third = from_third(lax.axis_size("beta"))

    @pl.when(third)
    def _():
        sigma_ref[...] = part_ref[...] + third_ref[...].astype(F32).T

    @pl.when(jnp.logical_not(third))
    def _():
        sigma_ref[...] = part_ref[...]


def call(kernel, outs, operands, flops, moved, scratch=()):
    many = isinstance(outs, (list, tuple))
    spec = pl.BlockSpec(memory_space=VMEM)
    return pl.pallas_call(
        kernel,
        out_shape=outs,
        in_specs=[spec] * len(operands),
        out_specs=[spec] * len(outs) if many else spec,
        scratch_shapes=list(scratch),
        compiler_params=pltpu.CompilerParams(vmem_limit_bytes=40 * 2**20),
        cost_estimate=pl.CostEstimate(flops=flops, bytes_accessed=moved, transcendentals=0),
    )(*operands)


def local(coeffs, requests, repl_slot, repl_sign, pair_integrals):
    rows, cols = coeffs.shape
    peers = lax.axis_size("alpha")
    chips = lax.axis_size("beta")
    wanted = requests[0]
    cap = wanted.shape[1]
    width = peers * cap
    pairs = repl_slot.shape[0]

    ask = call(
        ask_kernel,
        jax.ShapeDtypeStruct((peers, 3 * cap), jnp.int32),
        (wanted.T,),
        6 * peers * peers * cap,
        16 * peers * cap,
    )
    asked = lax.all_to_all(ask, "alpha", split_axis=0, concat_axis=0, tiled=True)
    asked_rows, asked_site = asked[:, :cap], asked[:, cap:]

    lanes = 1024 if (rows * pairs) % 1024 == 0 else rows * pairs
    group = 256 // pairs
    slot_rows = repl_slot.T.reshape(-1, lanes)
    sign_rows = repl_sign.T.reshape(-1, lanes)
    kron = jnp.kron(jnp.eye(group, dtype=BF16), pair_integrals.T)
    square = jax.ShapeDtypeStruct((width, width), BF16)
    high, low = call(
        coupling_kernel,
        [square, square],
        (slot_rows, sign_rows, kron),
        2 * rows * pairs * width * (width + 256),
        4 * width * width,
        scratch=[VMEM((width, width), F32)],
    )

    found = call(
        gather_kernel,
        jax.ShapeDtypeStruct((width, cols), BF16),
        (asked_rows, coeffs),
        2 * width * rows * cols,
        2 * (width + rows) * cols,
    )
    fetched = lax.all_to_all(
        found.reshape(peers, cap, cols), "alpha", split_axis=0, concat_axis=0, tiled=True
    ).reshape(width, cols)

    to_sites, to_owners = call(
        contributions_kernel,
        [jax.ShapeDtypeStruct((peers, 2 * cap, cols // 2), BF16), jax.ShapeDtypeStruct((width, cols), BF16)],
        (high, low, fetched),
        4 * width * width * cols,
        4 * width * width + 6 * width * cols,
    )

    def site_sums(to_sites):
        to_sites = lax.all_to_all(to_sites, "alpha", split_axis=0, concat_axis=0, tiled=True)
        return call(
            lambda *refs: site_kernel(cap, *refs),
            jax.ShapeDtypeStruct((cols, rows), BF16),
            (asked_site, to_sites.reshape(2 * width, cols // 2)),
            2 * cols * width * cols,
            2 * (width + rows) * cols,
        )

    def nothing(to_sites):
        return jnp.zeros((cols, rows), BF16)

    places = [], [], []
    for j in range(chips):
        for h in range(2):
            for z in range(chips):
                l = (j - z - h * (chips // 2)) % chips
                part = 1 if 2 * z >= chips else 0 if 2 * l >= chips else 2
                places[part].append(((2 * j + h) * chips + z, (2 * z + h) * chips + l))
    axes = ("alpha", "beta")
    is_first = lax.axis_index("beta") < chips // 2
    first = lax.cond(is_first, site_sums, nothing, to_sites)
    first, to_sites = lax.optimization_barrier((first, to_sites))
    second = lax.cond(is_first, nothing, site_sums, to_sites)
    to_owners, second = lax.optimization_barrier((to_owners, second))
    third = lax.ppermute(first, axes, places[2])
    first = lax.ppermute(first, axes, places[0])
    second = lax.ppermute(second, axes, places[1])
    to_owners = lax.all_to_all(
        to_owners.reshape(peers, cap, cols), "alpha", split_axis=0, concat_axis=0, tiled=True
    )
    block = jax.ShapeDtypeStruct((rows, cols), F32)
    first = call(turn_kernel, block, (first,), 15 * 10**8, 6 * rows * cols)
    turned = call(choose_kernel, block, (first, second), 32 * 10**8, 10 * rows * cols)
    part = call(
        own_kernel, block, (asked_rows, to_owners.reshape(width, cols), turned), 3 * 10**10, 10 * rows * cols
    )
    return call(sigma_kernel, block, (part, third), rows * cols, 10 * rows * cols)


def solution(mesh):
    in_specs = (P("alpha", "beta"), P("alpha", None, None), P(None, "alpha"), P(None, "alpha"), P())
    out_specs = P("alpha", "beta")
    return jax.shard_map(local, mesh=mesh, in_specs=in_specs, out_specs=out_specs, check_vma=False)
```

time: 87.2 us -> 82.8 us (0.950)
  the two profiles are of different devices: /device:TPU:320 before, /device:TPU:17 now
where the time goes in v2:
time: 82.8 us; the launch traced here: 82.3 us
  starting transfers between devices  26.1 us (32%)
  waiting for transfers between devices  24.2 us (29%)
  blocking collectives  15.3 us (18%)
  Pallas kernels  13.7 us (17%)
  local copies, waits for them, and re-layouts  2.58 us (3%)
    ppermute x1, waiting for transfers between devices, local(): second = lax.ppermute(second, axes, places[1])  19.5 us
    all_to_all x1, blocking collectives, site_sums(): lax.all_to_all(to_sites, 'alpha', split_axis=0, concat_axis=0, tiled=True)  15.3 us
    pallas_call x9, Pallas kernels, call(): pl.pallas_call(kernel, out_shape=outs, in_specs=[spec] * len(operands), o...  13.7 us
    all_to_all x1, starting transfers between devices, local(): lax.all_to_all(ask, 'alpha', split_axis=0, concat_axis=0, tiled=True)  9.74 us
    all_to_all x1, starting transfers between devices, local(): lax.all_to_all(found.reshape(peers, cap, cols), 'alpha', split_axis=0, co...  6.21 us
    all_to_all x1, starting transfers between devices, local(): lax.all_to_all(to_owners.reshape(peers, cap, cols), 'alpha', split_axis=0...  6.21 us
    all_to_all x1, waiting for transfers between devices, local(): lax.all_to_all(ask, 'alpha', split_axis=0, concat_axis=0, tiled=True)  2.99 us
    ppermute x1, starting transfers between devices, local(): third = lax.ppermute(first, axes, places[2])  1.99 us
  transfers between devices with their start and end apart: 6, of which 3 were waited for; matrix products, arithmetic and copies ran while one was open for 1% of the time, Pallas kernels for 11%

profile of v2, /device:TPU:17, one launch (start us, length us, event | category | flops | bytes accessed | tf_op | source)
XLA Modules:
  0.0 82.3 jit_solution(14758855525434963851)
XLA Ops:
  0.0 0.7 copy-done.1
  0.7 0.8 shard_map.55
  1.5 9.7 %all-to-all-start.2 = ((s32[32,1,48]{2,1,0:T(1,128)}), s32[32,1,48]{2,1,0:T(1,128)S(1)}, u32[]{:S(2)}, u32[]{:S(2)}) async-start(s32[32,1,48]{2,1,0:T(1,128)} %bitcast.5), calls=%async_computation.2 | async-start | bytes 32768 | tf_op jit(solution)/shard_map/all_to_all | solution.py:187
  11.5 0.4 mul.27.kron_ref
  11.9 0.4 copy-done.2
  12.5 0.5 copy-done.3
  13.2 3.0 %all-to-all-done.2 = s32[32,1,48]{2,1,0:T(1,128)S(1)} async-done(((s32[32,1,48]{2,1,0:T(1,128)}), s32[32,1,48]{2,1,0:T(1,128)S(1)}, u32[]{:S(2)}, u32[]{:S(2)}) %all-to-all-start.2) | async-done | bytes 6176 | tf_op jit(solution)/shard_map/all_to_all | solution.py:187
  16.2 1.3 %shard_map.57 = bf16[512,512]{1,0:T(8,128)(2,1)} custom-call(s32[32,16]{1,0:T(8,128)S(1)} %bitcast.23, bf16[256,512]{1,0:T(8,128)(2,1)S(1)} %copy-done), custom_call_target="tpu_custom_call" | custom-call | flops 134217728 | bytes 786432 | tf_op jit(solution)/shard_map/pallas_call | solution.py:160
  17.5 6.2 %all-to-all-start.3 = ((bf16[32,16,512]{2,1,0:T(8,128)(2,1)}), bf16[32,16,512]{2,1,0:T(8,128)(2,1)S(1)}, u32[]{:S(2)}, u32[]{:S(2)}) async-start(bf16[32,16,512]{2,1,0:T(8,128)(2,1)} %bitcast.10), calls=%async_computation.3 | async-start | bytes 1048576 | tf_op jit(solution)/shard_map/all_to_all | solution.py:212
  23.7 8.1 %shard_map.56 = (bf16[512,512]{1,0:T(8,128)(2,1)S(1)}, bf16[512,512]{1,0:T(8,128)(2,1)S(1)}) custom-call(s32[8,1024]{1,0:T(8,128)S(1)} %reshape.40.slot_ref, s32[8,1024]{1,0:T(8,128)S(1)} %reshape.41.sign_ref, bf16[256,256]{1,0:T(8,128)(2,1)S(1)} %mul.27.kron_ref), custom_call_target="tpu_custom_call" | custom-call | flops 6442450944 | bytes 1048576 | tf_op jit(solution)/shard_map/pallas_call | solution.py:160
  31.9 1.7 %all-to-all-done.3 = bf16[32,16,512]{2,1,0:T(8,128)(2,1)S(1)} async-done(((bf16[32,16,512]{2,1,0:T(8,128)(2,1)}), bf16[32,16,512]{2,1,0:T(8,128)(2,1)S(1)}, u32[]{:S(2)}, u32[]{:S(2)}) %all-to-all-start.3) | async-done | bytes 524320 | tf_op jit(solution)/shard_map/all_to_all | solution.py:212
  33.6 1.5 %shard_map.58 = (bf16[32,32,256]{2,1,0:T(8,128)(2,1)S(1)}, bf16[512,512]{1,0:T(8,128)(2,1)}) custom-call(bf16[512,512]{1,0:T(8,128)(2,1)S(1)} %get-tuple-element.31.high_ref, bf16[512,512]{1,0:T(8,128)(2,1)S(1)} %get-tuple-element.32.low_ref, bf16[512,512]{1,0:T(8,128)(2,1)S(1)} %bitcast.20), custom_call_target="tpu_custom_call" | custom-call | flops 536870912 | bytes 2621440 | tf_op jit(solution)/shard_map/pallas_call | solution.py:160
  35.1 15.9 %conditional.2 = (bf16[512,256]{1,0:T(8,128)(2,1)S(1)}) conditional(s32[]{:T(128)} %convert_element_type.12, () %tuple.19, (bf16[32,32,256]{2,1,0:T(8,128)(2,1)S(1)}, s32[32,32]{1,0:T(8,128)S(1)}) %tuple.20), branch_computations={%region_0.1_spmd, %region_1.2_spmd} | conditional | flops 268435456 | bytes 1835016 | solution.py:246
  35.1 15.3 %all_to_all.30 = bf16[32,32,256]{2,1,0:T(8,128)(2,1)S(1)} all-to-all(bf16[32,32,256]{2,1,0:T(8,128)(2,1)S(1)} %get-tuple-element.20), channel_id=1, replica_groups=mesh['alpha'=32,'beta'=16] {'alpha'}, dimensions={0} | all-to-all | bytes 1048576 | tf_op jit(solution)/shard_map/cond/branch_1_fun/all_to_all | solution.py:225
  50.4 0.6 branch_1_fun.1
  51.0 0.7 collective-permute-start
  51.7 1.3 %collective-permute-start.1 = (bf16[512,256]{1,0:T(8,128)(2,1)S(1)}, bf16[512,256]{1,0:T(8,128)(2,1)S(1)}, u32[]{:S(2)}, u32[]{:S(2)}) collective-permute-start(bf16[512,256]{1,0:T(8,128)(2,1)S(1)} %get-tuple-element.40), channel_id=1, source_target_pairs={{8,264},{9,295},{10,326},{11,357},{12,388},{13,419},{14,450},{15,4... | collective-permute-start | bytes 786440 | tf_op jit(solution)/shard_map/ppermute | solution.py:252
  53.0 6.2 %all-to-all-start.4 = ((bf16[32,16,512]{2,1,0:T(8,128)(2,1)}), bf16[32,16,512]{2,1,0:T(8,128)(2,1)S(1)}, u32[]{:S(2)}, u32[]{:S(2)}) async-start(bf16[32,16,512]{2,1,0:T(8,128)(2,1)} %bitcast.12), calls=%async_computation.4 | async-start | bytes 1048576 | tf_op jit(solution)/shard_map/all_to_all | solution.py:253
  59.2 2.0 %collective-permute-start.2 = (bf16[512,256]{1,0:T(8,128)(2,1)S(1)}, bf16[512,256]{1,0:T(8,128)(2,1)S(1)}, u32[]{:S(2)}, u32[]{:S(2)}) collective-permute-start(bf16[512,256]{1,0:T(8,128)(2,1)S(1)} %get-tuple-element.39), channel_id=1, source_target_pairs={{0,0},{17,55},{18,86},{19,117},{20,148},{21,179},{22,210},{23,241}... | collective-permute-start | bytes 786440 | tf_op jit(solution)/shard_map/ppermute | solution.py:250
  61.2 0.1 shard_map.59.first_ref
  61.4 19.5 %collective-permute-done.1.second_ref = bf16[512,256]{1,0:T(8,128)(2,1)S(1)} collective-permute-done((bf16[512,256]{1,0:T(8,128)(2,1)S(1)}, bf16[512,256]{1,0:T(8,128)(2,1)S(1)}, u32[]{:S(2)}, u32[]{:S(2)}) %collective-permute-start.1) | collective-permute-done | bytes 262176 | tf_op jit(solution)/shard_map/ppermute | solution.py:252
  80.9 0.1 shard_map.60.turned_ref
  81.0 0.4 shard_map.61.part_ref
  81.4 0.8 %shard_map.62 = f32[256,512]{1,0:T(8,128)} custom-call(f32[256,512]{1,0:T(8,128)S(1)} %shard_map.61.part_ref, bf16[512,256]{1,0:T(8,128)(2,1)S(1)} %collective-permute-done.2.third_ref), custom_call_target="tpu_custom_call" | custom-call | flops 131072 | bytes 1310720 | tf_op jit(solution)/shard_map/pallas_call | solution.py:160
  (20 shorter events, 0.8 us)
Async XLA Ops:
  0.0 0.7 copy-start.1
  1.5 9.8 %copy-start.4 = (bf16[32,32]{1,0:T(8,128)(2,1)S(1)}, bf16[32,32]{1,0:T(8,128)(2,1)}, u32[]{:S(2)}) copy-start(bf16[32,32]{1,0:T(8,128)(2,1)} %param.13) | copy-start | bytes 6148
  1.5 14.7 %all-to-all-start.2 = ((s32[32,1,48]{2,1,0:T(1,128)}), s32[32,1,48]{2,1,0:T(1,128)S(1)}, u32[]{:S(2)}, u32[]{:S(2)}) async-start(s32[32,1,48]{2,1,0:T(1,128)} %bitcast.5), calls=%async_computation.2 | async-start | bytes 32768 | tf_op jit(solution)/shard_map/all_to_all | solution.py:187
  11.5 0.8 copy-start.2
  12.2 0.8 copy-start.3
  12.3 3.9 %copy-start = (bf16[256,512]{1,0:T(8,128)(2,1)S(1)}, bf16[256,512]{1,0:T(8,128)(2,1)}, u32[]{:S(2)}) copy-start(bf16[256,512]{1,0:T(8,128)(2,1)} %coeffs_ref.1) | copy-start | bytes 786436
  17.5 16.1 %all-to-all-start.3 = ((bf16[32,16,512]{2,1,0:T(8,128)(2,1)}), bf16[32,16,512]{2,1,0:T(8,128)(2,1)S(1)}, u32[]{:S(2)}, u32[]{:S(2)}) async-start(bf16[32,16,512]{2,1,0:T(8,128)(2,1)} %bitcast.10), calls=%async_computation.3 | async-start | bytes 1048576 | tf_op jit(solution)/shard_map/all_to_all | solution.py:212
  51.0 10.3 %collective-permute-start = (bf16[512,256]{1,0:T(8,128)(2,1)S(1)}, bf16[512,256]{1,0:T(8,128)(2,1)S(1)}, u32[]{:S(2)}, u32[]{:S(2)}) collective-permute-start(bf16[512,256]{1,0:T(8,128)(2,1)S(1)} %get-tuple-element.39), channel_id=1, source_target_pairs={{1,47},{2,78},{3,109},{4,140},{5,171},{6,202},{7,233},{16,24},{34,... | collective-permute-start | bytes 786440 | tf_op jit(solution)/shard_map/ppermute | solution.py:251
  51.7 29.2 %collective-permute-start.1 = (bf16[512,256]{1,0:T(8,128)(2,1)S(1)}, bf16[512,256]{1,0:T(8,128)(2,1)S(1)}, u32[]{:S(2)}, u32[]{:S(2)}) collective-permute-start(bf16[512,256]{1,0:T(8,128)(2,1)S(1)} %get-tuple-element.40), channel_id=1, source_target_pairs={{8,264},{9,295},{10,326},{11,357},{12,388},{13,419},{14,450},{15,4... | collective-permute-start | bytes 786440 | tf_op jit(solution)/shard_map/ppermute | solution.py:252
  53.0 28.0 %all-to-all-start.4 = ((bf16[32,16,512]{2,1,0:T(8,128)(2,1)}), bf16[32,16,512]{2,1,0:T(8,128)(2,1)S(1)}, u32[]{:S(2)}, u32[]{:S(2)}) async-start(bf16[32,16,512]{2,1,0:T(8,128)(2,1)} %bitcast.12), calls=%async_computation.4 | async-start | bytes 1048576 | tf_op jit(solution)/shard_map/all_to_all | solution.py:253
  59.2 22.2 %collective-permute-start.2 = (bf16[512,256]{1,0:T(8,128)(2,1)S(1)}, bf16[512,256]{1,0:T(8,128)(2,1)S(1)}, u32[]{:S(2)}, u32[]{:S(2)}) collective-permute-start(bf16[512,256]{1,0:T(8,128)(2,1)S(1)} %get-tuple-element.39), channel_id=1, source_target_pairs={{0,0},{17,55},{18,86},{19,117},{20,148},{21,179},{22,210},{23,241}... | collective-permute-start | bytes 786440 | tf_op jit(solution)/shard_map/ppermute | solution.py:250

commit v3 on v2

--- a/solution.py
+++ b/solution.py
@@ -27,7 +27,8 @@
     return (lines == row).astype(F32).astype(BF16)
 
 
-def ask_kernel(wanted_ref, ask_ref):
+def ask_kernel(from_ref, ask_ref, wanted_ref):
+    pltpu.sync_copy(from_ref, wanted_ref)
     cap, peers = wanted_ref.shape
     chips = peers // 2
     plane = lax.axis_index("beta")
@@ -77,17 +78,27 @@
     low_ref[...] = (total_ref[...] - high.astype(F32)).astype(BF16)
 
 
-def gather_kernel(asked_ref, coeffs_ref, found_ref):
+def gather_kernel(asked_ref, coeffs_ref, found_ref, held_ref, sems):
     rows = coeffs_ref.shape[0]
     peers, cap = asked_ref.shape
+    pieces = sems.shape[0]
     line = lax.broadcasted_iota(jnp.int32, (cap, cap), 0)
     same = (line == lax.broadcasted_iota(jnp.int32, (cap, cap), 1)).astype(F32).astype(BF16)
     asked = asked_ref[...].astype(F32).astype(BF16)
     asked = lax.dot_general(same, asked, (((1,), (1,)), ((), ())), preferred_element_type=F32)
     lane = lax.broadcasted_iota(jnp.int32, (cap, rows), 1).astype(F32)
-    table = [(asked[:, t : t + 1] == lane).astype(F32).astype(BF16) for t in range(peers)]
-    found = jnp.dot(jnp.concatenate(table, axis=0), coeffs_ref[...], preferred_element_type=F32)
-    found_ref[...] = found.astype(BF16)
+    step = peers // pieces
+    copies = []
+    for n in range(pieces):
+        tiles = range(n * step, (n + 1) * step)
+        table = [(asked[:, t : t + 1] == lane).astype(F32).astype(BF16) for t in tiles]
+        found = jnp.dot(jnp.concatenate(table, axis=0), coeffs_ref[...], preferred_element_type=F32)
+        piece = pl.ds(n * step * cap, step * cap)
+        held_ref[piece, :] = found.astype(BF16)
+        copies.append(pltpu.make_async_copy(held_ref.at[piece, :], found_ref.at[piece, :], sems.at[n]))
+        copies[n].start()
+    for copy in copies:
+        copy.wait()
 
 
 def contributions_kernel(high_ref, low_ref, fetched_ref, sites_ref, owners_ref):
@@ -114,6 +125,10 @@
     sent_ref[...] = jnp.dot(table, contrib_ref[...], preferred_element_type=F32).astype(BF16)
 
 
+def copy_kernel(from_ref, to_ref):
+    to_ref[...] = from_ref[...]
+
+
 def turn_kernel(sent_ref, turned_ref):
     turned_ref[...] = sent_ref[...].astype(F32).T
 
@@ -142,27 +157,25 @@
     part_ref[...] = jnp.dot(table, contrib_ref[...], preferred_element_type=F32) + turned_ref[...]
 
 
-def sigma_kernel(part_ref, third_ref, sigma_ref):
-    third = from_third(lax.axis_size("beta"))
-
-    @pl.when(third)
+def sigma_kernel(part_ref, third_ref, sigma_ref, held_ref):
+    @pl.when(from_third(lax.axis_size("beta")))
     def _():
-        sigma_ref[...] = part_ref[...] + third_ref[...].astype(F32).T
-
-    @pl.when(jnp.logical_not(third))
-    def _():
-        sigma_ref[...] = part_ref[...]
-
-
-def call(kernel, outs, operands, flops, moved, scratch=()):
+        pltpu.sync_copy(part_ref, held_ref)
+        held_ref[...] += third_ref[...].astype(F32).T
+        pltpu.sync_copy(held_ref, sigma_ref)
+
+
+def call(kernel, outs, operands, flops, moved, scratch=(), spaces=(), aliases=None, out_space=VMEM):
     many = isinstance(outs, (list, tuple))
-    spec = pl.BlockSpec(memory_space=VMEM)
+    spec = pl.BlockSpec(memory_space=out_space)
+    spaces = tuple(spaces) + (VMEM,) * (len(operands) - len(spaces))
     return pl.pallas_call(
         kernel,
         out_shape=outs,
-        in_specs=[spec] * len(operands),
+        in_specs=[pl.BlockSpec(memory_space=space) for space in spaces],
         out_specs=[spec] * len(outs) if many else spec,
         scratch_shapes=list(scratch),
+        input_output_aliases=aliases or {},
         compiler_params=pltpu.CompilerParams(vmem_limit_bytes=40 * 2**20),
         cost_estimate=pl.CostEstimate(flops=flops, bytes_accessed=moved, transcendentals=0),
     )(*operands)
@@ -180,9 +193,11 @@
     ask = call(
         ask_kernel,
         jax.ShapeDtypeStruct((peers, 3 * cap), jnp.int32),
-        (wanted.T,),
+        (pltpu.with_memory_space_constraint(wanted.T, pltpu.HBM),),
         6 * peers * peers * cap,
         16 * peers * cap,
+        scratch=[VMEM((cap, peers), jnp.int32)],
+        spaces=[pltpu.HBM],
     )
     asked = lax.all_to_all(ask, "alpha", split_axis=0, concat_axis=0, tiled=True)
     asked_rows, asked_site = asked[:, :cap], asked[:, cap:]
@@ -208,6 +223,8 @@
         (asked_rows, coeffs),
         2 * width * rows * cols,
         2 * (width + rows) * cols,
+        scratch=[VMEM((width, cols), BF16), pltpu.SemaphoreType.DMA((4,))],
+        out_space=pl.ANY,
     )
     fetched = lax.all_to_all(
         found.reshape(peers, cap, cols), "alpha", split_axis=0, concat_axis=0, tiled=True
@@ -250,6 +267,7 @@
     third = lax.ppermute(first, axes, places[2])
     first = lax.ppermute(first, axes, places[0])
     second = lax.ppermute(second, axes, places[1])
+    to_owners = call(copy_kernel, jax.ShapeDtypeStruct((width, cols), BF16), (to_owners,), 0, 4 * width * cols)
     to_owners = lax.all_to_all(
         to_owners.reshape(peers, cap, cols), "alpha", split_axis=0, concat_axis=0, tiled=True
     )
@@ -257,9 +275,23 @@
     first = call(turn_kernel, block, (first,), 15 * 10**8, 6 * rows * cols)
     turned = call(choose_kernel, block, (first, second), 32 * 10**8, 10 * rows * cols)
     part = call(
-        own_kernel, block, (asked_rows, to_owners.reshape(width, cols), turned), 3 * 10**10, 10 * rows * cols
-    )
-    return call(sigma_kernel, block, (part, third), rows * cols, 10 * rows * cols)
+        own_kernel,
+        block,
+        (asked_rows, to_owners.reshape(width, cols), turned),
+        3 * 10**10,
+        10 * rows * cols,
+    )
+    return call(
+        sigma_kernel,
+        block,
+        (part, third),
+        rows * cols,
+        10 * rows * cols,
+        scratch=[VMEM((rows, cols), F32)],
+        spaces=[pl.ANY],
+        aliases={0: 0},
+        out_space=pl.ANY,
+    )
 
 
 def solution(mesh):

time: 82.8 us -> 82.2 us (level)
  the two profiles are of different devices: /device:TPU:17 before, /device:TPU:73 now
where the time goes in v3:
time: 82.2 us; the launch traced here: 81.6 us
  waiting for transfers between devices  25.6 us (31%)
  starting transfers between devices  22.2 us (27%)
  Pallas kernels  16.3 us (20%)
  blocking collectives  15.3 us (19%)
  local copies, waits for them, and re-layouts  1.88 us (2%)
    pallas_call x10, Pallas kernels, call(): pl.pallas_call(kernel, out_shape=outs, in_specs=[pl.BlockSpec(memory_spac...  16.3 us
    all_to_all x1, blocking collectives, site_sums(): lax.all_to_all(to_sites, 'alpha', split_axis=0, concat_axis=0, tiled=True)  15.3 us
    all_to_all x1, waiting for transfers between devices, local(): lax.all_to_all(to_owners.reshape(peers, cap, cols), 'alpha', split_axis=0...  14.5 us
    all_to_all x1, starting transfers between devices, local(): lax.all_to_all(ask, 'alpha', split_axis=0, concat_axis=0, tiled=True)  7.98 us
    all_to_all x1, starting transfers between devices, local(): lax.all_to_all(to_owners.reshape(peers, cap, cols), 'alpha', split_axis=0...  5.69 us
    all_to_all x1, starting transfers between devices, local(): lax.all_to_all(found.reshape(peers, cap, cols), 'alpha', split_axis=0, co...  5.3 us
    ppermute x1, waiting for transfers between devices, local(): third = lax.ppermute(first, axes, places[2])  4.98 us
    all_to_all x1, waiting for transfers between devices, local(): lax.all_to_all(ask, 'alpha', split_axis=0, concat_axis=0, tiled=True)  3.85 us
  transfers between devices with their start and end apart: 6, of which 4 were waited for; matrix products, arithmetic and copies ran while one was open for 1% of the time, Pallas kernels for 13%

profile of v3, /device:TPU:73, one launch (start us, length us, event | category | flops | bytes accessed | tf_op | source)
XLA Modules:
  0.0 81.6 jit_solution(11511524572971396949)
XLA Ops:
  0.0 1.5 %shard_map.55 = s32[32,48]{1,0:T(8,128)} custom-call(s32[16,32]{1,0:T(8,128)} %bitcast.28), custom_call_target="tpu_custom_call" | custom-call | flops 98304 | bytes 8192 | tf_op jit(solution)/shard_map/pallas_call | solution.py:172
  1.5 8.0 %all-to-all-start.2 = ((s32[32,1,48]{2,1,0:T(1,128)}), s32[32,1,48]{2,1,0:T(1,128)S(1)}, u32[]{:S(2)}, u32[]{:S(2)}) async-start(s32[32,1,48]{2,1,0:T(1,128)} %bitcast.5), calls=%async_computation.2 | async-start | bytes 32768 | tf_op jit(solution)/shard_map/all_to_all | solution.py:202
  9.7 0.4 mul.27.kron_ref
  10.1 0.4 copy-done.1
  10.7 0.5 copy-done.2
  11.5 3.9 %all-to-all-done.2 = s32[32,1,48]{2,1,0:T(1,128)S(1)} async-done(((s32[32,1,48]{2,1,0:T(1,128)}), s32[32,1,48]{2,1,0:T(1,128)S(1)}, u32[]{:S(2)}, u32[]{:S(2)}) %all-to-all-start.2) | async-done | bytes 6176 | tf_op jit(solution)/shard_map/all_to_all | solution.py:202
  15.3 1.2 %shard_map.57 = bf16[512,512]{1,0:T(8,128)(2,1)} custom-call(s32[32,16]{1,0:T(8,128)S(1)} %bitcast.23, bf16[256,512]{1,0:T(8,128)(2,1)S(1)} %copy-done), custom_call_target="tpu_custom_call" | custom-call | flops 134217728 | bytes 786432 | tf_op jit(solution)/shard_map/pallas_call | solution.py:172
  16.5 5.3 %all-to-all-start.3 = ((bf16[32,16,512]{2,1,0:T(8,128)(2,1)}), bf16[32,16,512]{2,1,0:T(8,128)(2,1)S(1)}, u32[]{:S(2)}, u32[]{:S(2)}) async-start(bf16[32,16,512]{2,1,0:T(8,128)(2,1)} %bitcast.10), calls=%async_computation.3 | async-start | bytes 1048576 | tf_op jit(solution)/shard_map/all_to_all | solution.py:229
  21.8 8.1 %shard_map.56 = (bf16[512,512]{1,0:T(8,128)(2,1)S(1)}, bf16[512,512]{1,0:T(8,128)(2,1)S(1)}) custom-call(s32[8,1024]{1,0:T(8,128)S(1)} %reshape.40.slot_ref, s32[8,1024]{1,0:T(8,128)S(1)} %reshape.41.sign_ref, bf16[256,256]{1,0:T(8,128)(2,1)S(1)} %mul.27.kron_ref), custom_call_target="tpu_custom_call" | custom-call | flops 6442450944 | bytes 1048576 | tf_op jit(solution)/shard_map/pallas_call | solution.py:172
  30.0 2.2 %all-to-all-done.3 = bf16[32,16,512]{2,1,0:T(8,128)(2,1)S(1)} async-done(((bf16[32,16,512]{2,1,0:T(8,128)(2,1)}), bf16[32,16,512]{2,1,0:T(8,128)(2,1)S(1)}, u32[]{:S(2)}, u32[]{:S(2)}) %all-to-all-start.3) | async-done | bytes 524320 | tf_op jit(solution)/shard_map/all_to_all | solution.py:229
  32.2 0.7 shard_map.58
  33.0 15.9 %conditional.2 = (bf16[512,256]{1,0:T(8,128)(2,1)S(1)}) conditional(s32[]{:T(128)} %convert_element_type.12, () %tuple.19, (bf16[32,32,256]{2,1,0:T(8,128)(2,1)S(1)}, s32[32,32]{1,0:T(8,128)S(1)}) %tuple.20), branch_computations={%region_0.1_spmd, %region_1.2_spmd} | conditional | flops 268435456 | bytes 1835016 | solution.py:263
  33.0 15.3 %all_to_all.30 = bf16[32,32,256]{2,1,0:T(8,128)(2,1)S(1)} all-to-all(bf16[32,32,256]{2,1,0:T(8,128)(2,1)S(1)} %get-tuple-element.20), channel_id=1, replica_groups=mesh['alpha'=32,'beta'=16] {'alpha'}, dimensions={0} | all-to-all | bytes 1048576 | tf_op jit(solution)/shard_map/cond/branch_1_fun/all_to_all | solution.py:242
  48.3 0.6 branch_1_fun.1
  48.9 1.3 %collective-permute-start = (bf16[512,256]{1,0:T(8,128)(2,1)S(1)}, bf16[512,256]{1,0:T(8,128)(2,1)S(1)}, u32[]{:S(2)}, u32[]{:S(2)}) collective-permute-start(bf16[512,256]{1,0:T(8,128)(2,1)S(1)} %get-tuple-element.39), channel_id=1, source_target_pairs={{1,47},{2,78},{3,109},{4,140},{5,171},{6,202},{7,233},{16,24},{34,... | collective-permute-start | bytes 786440 | tf_op jit(solution)/shard_map/ppermute | solution.py:268
  50.3 0.7 collective-permute-start.1
  51.0 0.8 %shard_map.59 = bf16[512,512]{1,0:T(8,128)(2,1)} custom-call(bf16[512,512]{1,0:T(8,128)(2,1)S(1)} %get-tuple-element.36.from_ref), custom_call_target="tpu_custom_call" | custom-call | bytes 1048576 | tf_op jit(solution)/shard_map/pallas_call | solution.py:172
  51.8 5.7 %all-to-all-start.4 = ((bf16[32,16,512]{2,1,0:T(8,128)(2,1)}), bf16[32,16,512]{2,1,0:T(8,128)(2,1)S(1)}, u32[]{:S(2)}, u32[]{:S(2)}) async-start(bf16[32,16,512]{2,1,0:T(8,128)(2,1)} %bitcast.12), calls=%async_computation.4 | async-start | bytes 1048576 | tf_op jit(solution)/shard_map/all_to_all | solution.py:271
  57.5 1.3 %collective-permute-start.2 = (bf16[512,256]{1,0:T(8,128)(2,1)S(1)}, bf16[512,256]{1,0:T(8,128)(2,1)S(1)}, u32[]{:S(2)}, u32[]{:S(2)}) collective-permute-start(bf16[512,256]{1,0:T(8,128)(2,1)S(1)} %get-tuple-element.39), channel_id=1, source_target_pairs={{0,0},{17,55},{18,86},{19,117},{20,148},{21,179},{22,210},{23,241}... | collective-permute-start | bytes 786440 | tf_op jit(solution)/shard_map/ppermute | solution.py:267
  58.8 0.1 shard_map.60.first_ref
  59.0 14.5 %all-to-all-done.4 = bf16[32,16,512]{2,1,0:T(8,128)(2,1)S(1)} async-done(((bf16[32,16,512]{2,1,0:T(8,128)(2,1)}), bf16[32,16,512]{2,1,0:T(8,128)(2,1)S(1)}, u32[]{:S(2)}, u32[]{:S(2)}) %all-to-all-start.4) | async-done | bytes 524320 | tf_op jit(solution)/shard_map/all_to_all | solution.py:271
  73.5 1.2 %shard_map.62.part_ref = f32[256,512]{1,0:T(8,128)} custom-call(s32[32,16]{1,0:T(8,128)S(1)} %bitcast.25, bf16[512,512]{1,0:T(8,128)(2,1)S(1)} %bitcast.19, f32[256,512]{1,0:T(8,128)S(1)} %shard_map.61.turned_ref), custom_call_target="tpu_custom_call" | custom-call | flops 30000001024 | bytes 1310720 | tf_op jit(solution)/shard_map/pallas_call | solution.py:172
  74.7 5.0 %collective-permute-done.2.third_ref = bf16[512,256]{1,0:T(8,128)(2,1)S(1)} collective-permute-done((bf16[512,256]{1,0:T(8,128)(2,1)S(1)}, bf16[512,256]{1,0:T(8,128)(2,1)S(1)}, u32[]{:S(2)}, u32[]{:S(2)}) %collective-permute-start.2) | collective-permute-done | bytes 262176 | tf_op jit(solution)/shard_map/ppermute | solution.py:267
  79.7 2.0 %shard_map.63 = f32[256,512]{1,0:T(8,128)} custom-call(f32[256,512]{1,0:T(8,128)} %shard_map.62.part_ref, bf16[512,256]{1,0:T(8,128)(2,1)S(1)} %collective-permute-done.2.third_ref), custom_call_target="tpu_custom_call", output_to_operand_aliasing={{}: (0, {})} | custom-call | flops 131072 | bytes 1310720 | tf_op jit(solution)/shard_map/pallas_call | solution.py:172
  (19 shorter events, 0.8 us)
Async XLA Ops:
  1.5 8.0 %copy-start.3 = (bf16[32,32]{1,0:T(8,128)(2,1)S(1)}, bf16[32,32]{1,0:T(8,128)(2,1)}, u32[]{:S(2)}) copy-start(bf16[32,32]{1,0:T(8,128)(2,1)} %param.13) | copy-start | bytes 6148
  1.5 13.8 %all-to-all-start.2 = ((s32[32,1,48]{2,1,0:T(1,128)}), s32[32,1,48]{2,1,0:T(1,128)S(1)}, u32[]{:S(2)}, u32[]{:S(2)}) async-start(s32[32,1,48]{2,1,0:T(1,128)} %bitcast.5), calls=%async_computation.2 | async-start | bytes 32768 | tf_op jit(solution)/shard_map/all_to_all | solution.py:202
  9.7 0.8 copy-start.1
  10.5 0.8 copy-start.2
  10.6 4.7 %copy-start = (bf16[256,512]{1,0:T(8,128)(2,1)S(1)}, bf16[256,512]{1,0:T(8,128)(2,1)}, u32[]{:S(2)}) copy-start(bf16[256,512]{1,0:T(8,128)(2,1)} %coeffs_ref.1) | copy-start | bytes 786436
  16.5 15.7 %all-to-all-start.3 = ((bf16[32,16,512]{2,1,0:T(8,128)(2,1)}), bf16[32,16,512]{2,1,0:T(8,128)(2,1)S(1)}, u32[]{:S(2)}, u32[]{:S(2)}) async-start(bf16[32,16,512]{2,1,0:T(8,128)(2,1)} %bitcast.10), calls=%async_computation.3 | async-start | bytes 1048576 | tf_op jit(solution)/shard_map/all_to_all | solution.py:229
  48.9 9.9 %collective-permute-start = (bf16[512,256]{1,0:T(8,128)(2,1)S(1)}, bf16[512,256]{1,0:T(8,128)(2,1)S(1)}, u32[]{:S(2)}, u32[]{:S(2)}) collective-permute-start(bf16[512,256]{1,0:T(8,128)(2,1)S(1)} %get-tuple-element.39), channel_id=1, source_target_pairs={{1,47},{2,78},{3,109},{4,140},{5,171},{6,202},{7,233},{16,24},{34,... | collective-permute-start | bytes 786440 | tf_op jit(solution)/shard_map/ppermute | solution.py:268
  50.3 8.7 %collective-permute-start.1 = (bf16[512,256]{1,0:T(8,128)(2,1)S(1)}, bf16[512,256]{1,0:T(8,128)(2,1)S(1)}, u32[]{:S(2)}, u32[]{:S(2)}) collective-permute-start(bf16[512,256]{1,0:T(8,128)(2,1)S(1)} %get-tuple-element.40), channel_id=1, source_target_pairs={{8,264},{9,295},{10,326},{11,357},{12,388},{13,419},{14,450},{15,4... | collective-permute-start | bytes 786440 | tf_op jit(solution)/shard_map/ppermute | solution.py:269
  51.8 21.7 %all-to-all-start.4 = ((bf16[32,16,512]{2,1,0:T(8,128)(2,1)}), bf16[32,16,512]{2,1,0:T(8,128)(2,1)S(1)}, u32[]{:S(2)}, u32[]{:S(2)}) async-start(bf16[32,16,512]{2,1,0:T(8,128)(2,1)} %bitcast.12), calls=%async_computation.4 | async-start | bytes 1048576 | tf_op jit(solution)/shard_map/all_to_all | solution.py:271
  57.5 22.2 %collective-permute-start.2 = (bf16[512,256]{1,0:T(8,128)(2,1)S(1)}, bf16[512,256]{1,0:T(8,128)(2,1)S(1)}, u32[]{:S(2)}, u32[]{:S(2)}) collective-permute-start(bf16[512,256]{1,0:T(8,128)(2,1)S(1)} %get-tuple-element.39), channel_id=1, source_target_pairs={{0,0},{17,55},{18,86},{19,117},{20,148},{21,179},{22,210},{23,241}... | collective-permute-start | bytes 786440 | tf_op jit(solution)/shard_map/ppermute | solution.py:267

commit v4 on v3

--- a/solution.py
+++ b/solution.py
@@ -23,8 +23,16 @@
 
 def one_hot(row, count):
     width = row.shape[1]
-    lines = lax.broadcasted_iota(jnp.int32, (count, width), 0).astype(F32)
-    return (lines == row).astype(F32).astype(BF16)
+    middle = count // 2
+    row = jnp.broadcast_to(row - middle, (16, width)).astype(BF16)
+    line = lax.broadcasted_iota(jnp.int32, (16, width), 0).astype(F32).astype(BF16)
+    one, zero = jnp.ones((16, width), BF16), jnp.zeros((16, width), BF16)
+    lines = [jnp.where(row == line + jnp.asarray(n - middle, BF16), one, zero) for n in range(0, count, 16)]
+    return jnp.concatenate(lines, axis=0)
+
+
+def early_planes(chips):
+    return 3 * chips // 8
 
 
 def ask_kernel(from_ref, ask_ref, wanted_ref):
@@ -34,7 +42,7 @@
     plane = lax.axis_index("beta")
     site = lax.broadcasted_iota(jnp.int32, (peers, peers), 0)
     tile = lax.broadcasted_iota(jnp.int32, (peers, peers), 1)
-    chip = site // 2 - plane - (site % 2) * (chips // 2)
+    chip = site // 2 - plane - (site % 2) * (chips // 2 - 1)
     chip = jnp.where(chip < 0, chip + chips, chip)
     chip = jnp.where(chip < 0, chip + chips, chip)
     wanted = wanted_ref[...].astype(F32).astype(BF16)
@@ -72,7 +80,7 @@
         )
         return carry
 
-    lax.fori_loop(0, chunks, step, 0)
+    lax.fori_loop(0, chunks, step, 0, unroll=True)
     high = total_ref[...].astype(BF16)
     high_ref[...] = high
     low_ref[...] = (total_ref[...] - high.astype(F32)).astype(BF16)
@@ -86,12 +94,16 @@
     same = (line == lax.broadcasted_iota(jnp.int32, (cap, cap), 1)).astype(F32).astype(BF16)
     asked = asked_ref[...].astype(F32).astype(BF16)
     asked = lax.dot_general(same, asked, (((1,), (1,)), ((), ())), preferred_element_type=F32)
-    lane = lax.broadcasted_iota(jnp.int32, (cap, rows), 1).astype(F32)
+    lane = lax.broadcasted_iota(jnp.int32, (cap, rows), 1).astype(F32).astype(BF16)
+    one, zero = jnp.ones((cap, rows), BF16), jnp.zeros((cap, rows), BF16)
     step = peers // pieces
     copies = []
     for n in range(pieces):
         tiles = range(n * step, (n + 1) * step)
-        table = [(asked[:, t : t + 1] == lane).astype(F32).astype(BF16) for t in tiles]
+        table = [
+            jnp.where(jnp.broadcast_to(asked[:, t : t + 1], (cap, rows)).astype(BF16) == lane, one, zero)
+            for t in tiles
+        ]
         found = jnp.dot(jnp.concatenate(table, axis=0), coeffs_ref[...], preferred_element_type=F32)
         piece = pl.ds(n * step * cap, step * cap)
         held_ref[piece, :] = found.astype(BF16)
@@ -111,7 +123,7 @@
     owners_ref[...] = contrib.astype(BF16)
     for j in range(chips):
         for h in range(2):
-            chip = lax.rem(j + 2 * chips - plane - h * (chips // 2), chips)
+            chip = lax.rem(j + 2 * chips - plane - h * (chips // 2 - 1), chips)
             start = pl.multiple_of(chip * two_cap, two_cap)
             sites_ref[2 * j + h] = owners_ref[pl.ds(start, two_cap), h * half : (h + 1) * half]
 
@@ -129,18 +141,20 @@
     to_ref[...] = from_ref[...]
 
 
-def turn_kernel(sent_ref, turned_ref):
+def turn_kernel(sent_ref, asked_ref, turned_ref, table_ref):
     turned_ref[...] = sent_ref[...].astype(F32).T
+    rows = turned_ref.shape[0]
+    table_ref[...] = one_hot(flat_row(asked_ref[...], rows), rows)
 
 
 def from_third(chips):
     source, place = lax.axis_index("alpha") // 2, lax.axis_index("beta")
-    return jnp.logical_and(source < chips // 2, place < chips // 2)
+    return jnp.logical_and(source < early_planes(chips), place < early_planes(chips))
 
 
 def choose_kernel(first_ref, second_ref, turned_ref):
     chips = lax.axis_size("beta")
-    from_first = lax.axis_index("alpha") // 2 < chips // 2
+    from_first = lax.axis_index("alpha") // 2 < early_planes(chips)
 
     @pl.when(from_first)
     def _():
@@ -151,29 +165,30 @@
         turned_ref[...] = second_ref[...].astype(F32).T
 
 
-def own_kernel(asked_ref, contrib_ref, turned_ref, part_ref):
-    rows = part_ref.shape[0]
-    table = one_hot(flat_row(asked_ref[...], rows), rows)
-    part_ref[...] = jnp.dot(table, contrib_ref[...], preferred_element_type=F32) + turned_ref[...]
-
-
-def sigma_kernel(part_ref, third_ref, sigma_ref, held_ref):
+def own_kernel(table_ref, contrib_ref, turned_ref, part_ref, sigma_ref, sem):
+    part_ref[...] = jnp.dot(table_ref[...], contrib_ref[...], preferred_element_type=F32) + turned_ref[...]
+    copy = pltpu.make_async_copy(part_ref, sigma_ref, sem)
+    copy.start()
+    copy.wait()
+
+
+def sigma_kernel(before_ref, part_ref, third_ref, sigma_ref, held_ref):
     @pl.when(from_third(lax.axis_size("beta")))
     def _():
-        pltpu.sync_copy(part_ref, held_ref)
-        held_ref[...] += third_ref[...].astype(F32).T
+        held_ref[...] = part_ref[...] + third_ref[...].astype(F32).T
         pltpu.sync_copy(held_ref, sigma_ref)
 
 
 def call(kernel, outs, operands, flops, moved, scratch=(), spaces=(), aliases=None, out_space=VMEM):
     many = isinstance(outs, (list, tuple))
     spec = pl.BlockSpec(memory_space=out_space)
+    specs = [pl.BlockSpec(memory_space=space) for space in out_space] if isinstance(out_space, tuple) else None
     spaces = tuple(spaces) + (VMEM,) * (len(operands) - len(spaces))
     return pl.pallas_call(
         kernel,
         out_shape=outs,
         in_specs=[pl.BlockSpec(memory_space=space) for space in spaces],
-        out_specs=[spec] * len(outs) if many else spec,
+        out_specs=specs or ([spec] * len(outs) if many else spec),
         scratch_shapes=list(scratch),
         input_output_aliases=aliases or {},
         compiler_params=pltpu.CompilerParams(vmem_limit_bytes=40 * 2**20),
@@ -255,11 +270,11 @@
     for j in range(chips):
         for h in range(2):
             for z in range(chips):
-                l = (j - z - h * (chips // 2)) % chips
-                part = 1 if 2 * z >= chips else 0 if 2 * l >= chips else 2
+                l = (j - z - h * (chips // 2 - 1)) % chips
+                part = 1 if z >= early_planes(chips) else 0 if l >= early_planes(chips) else 2
                 places[part].append(((2 * j + h) * chips + z, (2 * z + h) * chips + l))
     axes = ("alpha", "beta")
-    is_first = lax.axis_index("beta") < chips // 2
+    is_first = lax.axis_index("beta") < early_planes(chips)
     first = lax.cond(is_first, site_sums, nothing, to_sites)
     first, to_sites = lax.optimization_barrier((first, to_sites))
     second = lax.cond(is_first, nothing, site_sums, to_sites)
@@ -272,19 +287,22 @@
         to_owners.reshape(peers, cap, cols), "alpha", split_axis=0, concat_axis=0, tiled=True
     )
     block = jax.ShapeDtypeStruct((rows, cols), F32)
-    first = call(turn_kernel, block, (first,), 15 * 10**8, 6 * rows * cols)
+    table = jax.ShapeDtypeStruct((rows, width), BF16)
+    first, table = call(turn_kernel, [block, table], (first, asked_rows), 15 * 10**8, 6 * rows * cols)
     turned = call(choose_kernel, block, (first, second), 32 * 10**8, 10 * rows * cols)
-    part = call(
+    part, sigma = call(
         own_kernel,
-        block,
-        (asked_rows, to_owners.reshape(width, cols), turned),
+        [block, block],
+        (table, to_owners.reshape(width, cols), turned),
         3 * 10**10,
         10 * rows * cols,
+        scratch=[pltpu.SemaphoreType.DMA(())],
+        out_space=(VMEM, pl.ANY),
     )
     return call(
         sigma_kernel,
         block,
-        (part, third),
+        (sigma, part, third),
         rows * cols,
         10 * rows * cols,
         scratch=[VMEM((rows, cols), F32)],

time: 82.2 us -> 81.3 us (0.989)
  the two profiles are of different devices: /device:TPU:73 before, /device:TPU:195 now
where the time goes in v4:
time: 81.3 us; the launch traced here: 80.8 us
  starting transfers between devices  29.4 us (36%)
  waiting for transfers between devices  21.6 us (27%)
  blocking collectives  14.8 us (18%)
  Pallas kernels  12.9 us (16%)
  local copies, waits for them, and re-layouts  1.88 us (2%)
    all_to_all x1, blocking collectives, site_sums(): lax.all_to_all(to_sites, 'alpha', split_axis=0, concat_axis=0, tiled=True)  14.8 us
    all_to_all x1, waiting for transfers between devices, local(): lax.all_to_all(to_owners.reshape(peers, cap, cols), 'alpha', split_axis=0...  13.7 us
    pallas_call x10, Pallas kernels, call(): pl.pallas_call(kernel, out_shape=outs, in_specs=[pl.BlockSpec(memory_spac...  12.9 us
    all_to_all x1, starting transfers between devices, local(): lax.all_to_all(to_owners.reshape(peers, cap, cols), 'alpha', split_axis=0...  12.5 us
    all_to_all x1, starting transfers between devices, local(): lax.all_to_all(ask, 'alpha', split_axis=0, concat_axis=0, tiled=True)  8.06 us
    all_to_all x1, starting transfers between devices, local(): lax.all_to_all(found.reshape(peers, cap, cols), 'alpha', split_axis=0, co...  5.29 us
    all_to_all x1, waiting for transfers between devices, local(): lax.all_to_all(found.reshape(peers, cap, cols), 'alpha', split_axis=0, co...  4.05 us
    all_to_all x1, waiting for transfers between devices, local(): lax.all_to_all(ask, 'alpha', split_axis=0, concat_axis=0, tiled=True)  3.83 us
  transfers between devices with their start and end apart: 6, of which 3 were waited for; matrix products, arithmetic and copies ran while one was open for 1% of the time, Pallas kernels for 12%

profile of v4, /device:TPU:195, one launch (start us, length us, event | category | flops | bytes accessed | tf_op | source)
XLA Modules:
  0.0 80.8 jit_solution(17758253340151750522)
XLA Ops:
  0.0 1.5 %shard_map.56 = s32[32,48]{1,0:T(8,128)} custom-call(s32[16,32]{1,0:T(8,128)} %bitcast.28), custom_call_target="tpu_custom_call" | custom-call | flops 98304 | bytes 8192 | tf_op jit(solution)/shard_map/pallas_call | solution.py:187
  1.5 8.1 %all-to-all-start.2 = ((s32[32,1,48]{2,1,0:T(1,128)}), s32[32,1,48]{2,1,0:T(1,128)S(1)}, u32[]{:S(2)}, u32[]{:S(2)}) async-start(s32[32,1,48]{2,1,0:T(1,128)} %bitcast.8), calls=%async_computation.2 | async-start | bytes 32768 | tf_op jit(solution)/shard_map/all_to_all | solution.py:217
  9.7 0.1 broadcast_multiply_fusion
  9.8 0.4 mul.27.kron_ref
  10.2 0.4 copy-done.1
  10.7 0.1 reshape.40.slot_ref
  10.8 0.5 copy-done.2
  11.5 3.8 %all-to-all-done.2 = s32[32,1,48]{2,1,0:T(1,128)S(1)} async-done(((s32[32,1,48]{2,1,0:T(1,128)}), s32[32,1,48]{2,1,0:T(1,128)S(1)}, u32[]{:S(2)}, u32[]{:S(2)}) %all-to-all-start.2) | async-done | bytes 6176 | tf_op jit(solution)/shard_map/all_to_all | solution.py:217
  15.4 1.2 %shard_map.57 = bf16[512,512]{1,0:T(8,128)(2,1)} custom-call(s32[32,16]{1,0:T(8,128)S(1)} %bitcast.23, bf16[256,512]{1,0:T(8,128)(2,1)S(1)} %copy-done), custom_call_target="tpu_custom_call" | custom-call | flops 134217728 | bytes 786432 | tf_op jit(solution)/shard_map/pallas_call | solution.py:187
  16.6 5.3 %all-to-all-start.3 = ((bf16[32,16,512]{2,1,0:T(8,128)(2,1)}), bf16[32,16,512]{2,1,0:T(8,128)(2,1)S(1)}, u32[]{:S(2)}, u32[]{:S(2)}) async-start(bf16[32,16,512]{2,1,0:T(8,128)(2,1)} %bitcast.10), calls=%async_computation.3 | async-start | bytes 1048576 | tf_op jit(solution)/shard_map/all_to_all | solution.py:244
  21.9 6.7 %shard_map.55 = (bf16[512,512]{1,0:T(8,128)(2,1)S(1)}, bf16[512,512]{1,0:T(8,128)(2,1)S(1)}) custom-call(s32[8,1024]{1,0:T(8,128)S(1)} %reshape.40.slot_ref, s32[8,1024]{1,0:T(8,128)S(1)} %reshape.41.sign_ref, bf16[256,256]{1,0:T(8,128)(2,1)S(1)} %mul.27.kron_ref), custom_call_target="tpu_custom_call" | custom-call | flops 6442450944 | bytes 1048576 | tf_op jit(solution)/shard_map/pallas_call | solution.py:187
  28.6 4.1 %all-to-all-done.3 = bf16[32,16,512]{2,1,0:T(8,128)(2,1)S(1)} async-done(((bf16[32,16,512]{2,1,0:T(8,128)(2,1)}), bf16[32,16,512]{2,1,0:T(8,128)(2,1)S(1)}, u32[]{:S(2)}, u32[]{:S(2)}) %all-to-all-start.3) | async-done | bytes 524320 | tf_op jit(solution)/shard_map/all_to_all | solution.py:244
  32.7 0.7 shard_map.58
  33.5 1.3 %collective-permute-start = (bf16[512,256]{1,0:T(8,128)(2,1)S(1)}, bf16[512,256]{1,0:T(8,128)(2,1)S(1)}, u32[]{:S(2)}, u32[]{:S(2)}) collective-permute-start(bf16[512,256]{1,0:T(8,128)(2,1)S(1)} %get-tuple-element.47), channel_id=1, source_target_pairs={{1,47},{2,78},{3,109},{4,140},{5,171},{16,25},{17,56},{18,87},{19,... | collective-permute-start | bytes 786440 | tf_op jit(solution)/shard_map/ppermute | solution.py:283
  34.8 15.3 %conditional.3 = (bf16[512,256]{1,0:T(8,128)(2,1)S(1)}) conditional(s32[]{:T(128)} %convert_element_type.11, (bf16[32,32,256]{2,1,0:T(8,128)(2,1)S(1)}, s32[32,32]{1,0:T(8,128)S(1)}) %tuple.22, () %tuple.23), branch_computations={%region_2.3_spmd, %region_3.4_spmd} | conditional | flops 268435456 | bytes 1835016 | solution.py:280
  34.8 14.8 %all_to_all.31 = bf16[32,32,256]{2,1,0:T(8,128)(2,1)S(1)} all-to-all(bf16[32,32,256]{2,1,0:T(8,128)(2,1)S(1)} %get-tuple-element.22), channel_id=1, replica_groups=mesh['alpha'=32,'beta'=16] {'alpha'}, dimensions={0} | all-to-all | bytes 1048576 | tf_op jit(solution)/shard_map/cond/branch_0_fun/all_to_all | solution.py:257
  49.5 0.6 branch_0_fun.1
  50.1 1.5 %collective-permute-start.1 = (bf16[512,256]{1,0:T(8,128)(2,1)S(1)}, bf16[512,256]{1,0:T(8,128)(2,1)S(1)}, u32[]{:S(2)}, u32[]{:S(2)}) collective-permute-start(bf16[512,256]{1,0:T(8,128)(2,1)S(1)} %get-tuple-element.48), channel_id=1, source_target_pairs={{6,202},{7,233},{8,264},{9,295},{10,326},{11,357},{12,388},{13,419... | collective-permute-start | bytes 786440 | tf_op jit(solution)/shard_map/ppermute | solution.py:284
  51.6 0.8 %shard_map.60 = bf16[512,512]{1,0:T(8,128)(2,1)} custom-call(bf16[512,512]{1,0:T(8,128)(2,1)S(1)} %get-tuple-element.42.from_ref), custom_call_target="tpu_custom_call" | custom-call | bytes 1048576 | tf_op jit(solution)/shard_map/pallas_call | solution.py:187
  52.5 12.5 %all-to-all-start.4 = ((bf16[32,16,512]{2,1,0:T(8,128)(2,1)}), bf16[32,16,512]{2,1,0:T(8,128)(2,1)S(1)}, u32[]{:S(2)}, u32[]{:S(2)}) async-start(bf16[32,16,512]{2,1,0:T(8,128)(2,1)} %bitcast.12), calls=%async_computation.4 | async-start | bytes 1048576 | tf_op jit(solution)/shard_map/all_to_all | solution.py:286
  65.0 0.7 collective-permute-start.2
  65.7 0.2 shard_map.59
  66.0 13.7 %all-to-all-done.4 = bf16[32,16,512]{2,1,0:T(8,128)(2,1)S(1)} async-done(((bf16[32,16,512]{2,1,0:T(8,128)(2,1)}), bf16[32,16,512]{2,1,0:T(8,128)(2,1)S(1)}, u32[]{:S(2)}, u32[]{:S(2)}) %all-to-all-start.4) | async-done | bytes 524320 | tf_op jit(solution)/shard_map/all_to_all | solution.py:286
  79.7 1.1 %shard_map.62 = (f32[256,512]{1,0:T(8,128)S(1)}, f32[256,512]{1,0:T(8,128)}) custom-call(bf16[256,512]{1,0:T(8,128)(2,1)S(1)} %get-tuple-element.39.table_ref, bf16[512,512]{1,0:T(8,128)(2,1)S(1)} %bitcast.19, f32[256,512]{1,0:T(8,128)S(1)} %shard_map.61.turned_ref), custom_call_target="tpu_custom_call" | custom-call | flops 30000001024 | bytes 1310720 | tf_op jit(solution)/shard_map/pallas_call | solution.py:187
  (19 shorter events, 0.6 us)
Async XLA Ops:
  1.5 8.1 %copy-start.3 = (bf16[32,32]{1,0:T(8,128)(2,1)S(1)}, bf16[32,32]{1,0:T(8,128)(2,1)}, u32[]{:S(2)}) copy-start(bf16[32,32]{1,0:T(8,128)(2,1)} %param.13) | copy-start | bytes 6148
  1.5 13.9 %all-to-all-start.2 = ((s32[32,1,48]{2,1,0:T(1,128)}), s32[32,1,48]{2,1,0:T(1,128)S(1)}, u32[]{:S(2)}, u32[]{:S(2)}) async-start(s32[32,1,48]{2,1,0:T(1,128)} %bitcast.8), calls=%async_computation.2 | async-start | bytes 32768 | tf_op jit(solution)/shard_map/all_to_all | solution.py:217
  9.8 0.8 copy-start.1
  10.6 0.8 copy-start.2
  10.7 4.7 %copy-start = (bf16[256,512]{1,0:T(8,128)(2,1)S(1)}, bf16[256,512]{1,0:T(8,128)(2,1)}, u32[]{:S(2)}) copy-start(bf16[256,512]{1,0:T(8,128)(2,1)} %coeffs_ref.1) | copy-start | bytes 786436
  16.6 16.1 %all-to-all-start.3 = ((bf16[32,16,512]{2,1,0:T(8,128)(2,1)}), bf16[32,16,512]{2,1,0:T(8,128)(2,1)S(1)}, u32[]{:S(2)}, u32[]{:S(2)}) async-start(bf16[32,16,512]{2,1,0:T(8,128)(2,1)} %bitcast.10), calls=%async_computation.3 | async-start | bytes 1048576 | tf_op jit(solution)/shard_map/all_to_all | solution.py:244
  33.5 32.2 %collective-permute-start = (bf16[512,256]{1,0:T(8,128)(2,1)S(1)}, bf16[512,256]{1,0:T(8,128)(2,1)S(1)}, u32[]{:S(2)}, u32[]{:S(2)}) collective-permute-start(bf16[512,256]{1,0:T(8,128)(2,1)S(1)} %get-tuple-element.47), channel_id=1, source_target_pairs={{1,47},{2,78},{3,109},{4,140},{5,171},{16,25},{17,56},{18,87},{19,... | collective-permute-start | bytes 786440 | tf_op jit(solution)/shard_map/ppermute | solution.py:283
  50.1 15.8 %collective-permute-start.1 = (bf16[512,256]{1,0:T(8,128)(2,1)S(1)}, bf16[512,256]{1,0:T(8,128)(2,1)S(1)}, u32[]{:S(2)}, u32[]{:S(2)}) collective-permute-start(bf16[512,256]{1,0:T(8,128)(2,1)S(1)} %get-tuple-element.48), channel_id=1, source_target_pairs={{6,202},{7,233},{8,264},{9,295},{10,326},{11,357},{12,388},{13,419... | collective-permute-start | bytes 786440 | tf_op jit(solution)/shard_map/ppermute | solution.py:284
  52.5 27.2 %all-to-all-start.4 = ((bf16[32,16,512]{2,1,0:T(8,128)(2,1)}), bf16[32,16,512]{2,1,0:T(8,128)(2,1)S(1)}, u32[]{:S(2)}, u32[]{:S(2)}) async-start(bf16[32,16,512]{2,1,0:T(8,128)(2,1)} %bitcast.12), calls=%async_computation.4 | async-start | bytes 1048576 | tf_op jit(solution)/shard_map/all_to_all | solution.py:286
  65.0 15.8 %collective-permute-start.2 = (bf16[512,256]{1,0:T(8,128)(2,1)S(1)}, bf16[512,256]{1,0:T(8,128)(2,1)S(1)}, u32[]{:S(2)}, u32[]{:S(2)}) collective-permute-start(bf16[512,256]{1,0:T(8,128)(2,1)S(1)} %get-tuple-element.47), channel_id=1, source_target_pairs={{0,0},{20,149},{21,180},{32,1},{33,32},{53,181},{64,2},{65,33},{66... | collective-permute-start | bytes 786440 | tf_op jit(solution)/shard_map/ppermute | solution.py:282

commit v5 on v4

--- a/solution.py
+++ b/solution.py
@@ -165,11 +165,18 @@
         turned_ref[...] = second_ref[...].astype(F32).T
 
 
-def own_kernel(table_ref, contrib_ref, turned_ref, part_ref, sigma_ref, sem):
-    part_ref[...] = jnp.dot(table_ref[...], contrib_ref[...], preferred_element_type=F32) + turned_ref[...]
-    copy = pltpu.make_async_copy(part_ref, sigma_ref, sem)
-    copy.start()
-    copy.wait()
+def own_kernel(table_ref, contrib_ref, turned_ref, part_ref, sigma_ref, sems):
+    rows = part_ref.shape[0]
+    step = rows // 2
+    copies = []
+    for n in range(2):
+        piece = pl.ds(n * step, step)
+        own = jnp.dot(table_ref[piece, :], contrib_ref[...], preferred_element_type=F32)
+        part_ref[piece, :] = own + turned_ref[piece, :]
+        copies.append(pltpu.make_async_copy(part_ref.at[piece, :], sigma_ref.at[piece, :], sems.at[n]))
+        copies[n].start()
+    for copy in copies:
+        copy.wait()
 
 
 def sigma_kernel(before_ref, part_ref, third_ref, sigma_ref, held_ref):
@@ -296,7 +303,7 @@
         (table, to_owners.reshape(width, cols), turned),
         3 * 10**10,
         10 * rows * cols,
-        scratch=[pltpu.SemaphoreType.DMA(())],
+        scratch=[pltpu.SemaphoreType.DMA((2,))],
         out_space=(VMEM, pl.ANY),
     )
     return call(

time: 81.3 us -> 81.3 us (level)
  no operation moved by 1% of the time
where the time goes in v5:
time: 81.3 us; the launch traced here: 80.7 us
  starting transfers between devices  29.4 us (36%)
  waiting for transfers between devices  21.6 us (27%)
  blocking collectives  14.8 us (18%)
  Pallas kernels  12.8 us (16%)
  local copies, waits for them, and re-layouts  1.88 us (2%)
    all_to_all x1, blocking collectives, site_sums(): lax.all_to_all(to_sites, 'alpha', split_axis=0, concat_axis=0, tiled=True)  14.8 us
    all_to_all x1, waiting for transfers between devices, local(): lax.all_to_all(to_owners.reshape(peers, cap, cols), 'alpha', split_axis=0...  13.7 us
    pallas_call x10, Pallas kernels, call(): pl.pallas_call(kernel, out_shape=outs, in_specs=[pl.BlockSpec(memory_spac...  12.8 us
    all_to_all x1, starting transfers between devices, local(): lax.all_to_all(to_owners.reshape(peers, cap, cols), 'alpha', split_axis=0...  12.5 us
    all_to_all x1, starting transfers between devices, local(): lax.all_to_all(ask, 'alpha', split_axis=0, concat_axis=0, tiled=True)  8.06 us
    all_to_all x1, starting transfers between devices, local(): lax.all_to_all(found.reshape(peers, cap, cols), 'alpha', split_axis=0, co...  5.29 us
    all_to_all x1, waiting for transfers between devices, local(): lax.all_to_all(found.reshape(peers, cap, cols), 'alpha', split_axis=0, co...  4.05 us
    all_to_all x1, waiting for transfers between devices, local(): lax.all_to_all(ask, 'alpha', split_axis=0, concat_axis=0, tiled=True)  3.83 us
  transfers between devices with their start and end apart: 6, of which 3 were waited for; matrix products, arithmetic and copies ran while one was open for 1% of the time, Pallas kernels for 12%

profile of v5, /device:TPU:195, one launch (start us, length us, event | category | flops | bytes accessed | tf_op | source)
XLA Modules:
  0.0 80.7 jit_solution(16975208902793863324)
XLA Ops:
  0.0 1.5 %shard_map.56 = s32[32,48]{1,0:T(8,128)} custom-call(s32[16,32]{1,0:T(8,128)} %bitcast.28), custom_call_target="tpu_custom_call" | custom-call | flops 98304 | bytes 8192 | tf_op jit(solution)/shard_map/pallas_call | solution.py:194
  1.5 8.1 %all-to-all-start.2 = ((s32[32,1,48]{2,1,0:T(1,128)}), s32[32,1,48]{2,1,0:T(1,128)S(1)}, u32[]{:S(2)}, u32[]{:S(2)}) async-start(s32[32,1,48]{2,1,0:T(1,128)} %bitcast.8), calls=%async_computation.2 | async-start | bytes 32768 | tf_op jit(solution)/shard_map/all_to_all | solution.py:224
  9.7 0.1 broadcast_multiply_fusion
  9.8 0.4 mul.27.kron_ref
  10.2 0.4 copy-done.1
  10.7 0.1 reshape.40.slot_ref
  10.8 0.5 copy-done.2
  11.5 3.8 %all-to-all-done.2 = s32[32,1,48]{2,1,0:T(1,128)S(1)} async-done(((s32[32,1,48]{2,1,0:T(1,128)}), s32[32,1,48]{2,1,0:T(1,128)S(1)}, u32[]{:S(2)}, u32[]{:S(2)}) %all-to-all-start.2) | async-done | bytes 6176 | tf_op jit(solution)/shard_map/all_to_all | solution.py:224
  15.4 1.2 %shard_map.57 = bf16[512,512]{1,0:T(8,128)(2,1)} custom-call(s32[32,16]{1,0:T(8,128)S(1)} %bitcast.23, bf16[256,512]{1,0:T(8,128)(2,1)S(1)} %copy-done), custom_call_target="tpu_custom_call" | custom-call | flops 134217728 | bytes 786432 | tf_op jit(solution)/shard_map/pallas_call | solution.py:194
  16.6 5.3 %all-to-all-start.3 = ((bf16[32,16,512]{2,1,0:T(8,128)(2,1)}), bf16[32,16,512]{2,1,0:T(8,128)(2,1)S(1)}, u32[]{:S(2)}, u32[]{:S(2)}) async-start(bf16[32,16,512]{2,1,0:T(8,128)(2,1)} %bitcast.10), calls=%async_computation.3 | async-start | bytes 1048576 | tf_op jit(solution)/shard_map/all_to_all | solution.py:251
  21.9 6.7 %shard_map.55 = (bf16[512,512]{1,0:T(8,128)(2,1)S(1)}, bf16[512,512]{1,0:T(8,128)(2,1)S(1)}) custom-call(s32[8,1024]{1,0:T(8,128)S(1)} %reshape.40.slot_ref, s32[8,1024]{1,0:T(8,128)S(1)} %reshape.41.sign_ref, bf16[256,256]{1,0:T(8,128)(2,1)S(1)} %mul.27.kron_ref), custom_call_target="tpu_custom_call" | custom-call | flops 6442450944 | bytes 1048576 | tf_op jit(solution)/shard_map/pallas_call | solution.py:194
  28.6 4.1 %all-to-all-done.3 = bf16[32,16,512]{2,1,0:T(8,128)(2,1)S(1)} async-done(((bf16[32,16,512]{2,1,0:T(8,128)(2,1)}), bf16[32,16,512]{2,1,0:T(8,128)(2,1)S(1)}, u32[]{:S(2)}, u32[]{:S(2)}) %all-to-all-start.3) | async-done | bytes 524320 | tf_op jit(solution)/shard_map/all_to_all | solution.py:251
  32.7 0.7 shard_map.58
  33.5 1.3 %collective-permute-start = (bf16[512,256]{1,0:T(8,128)(2,1)S(1)}, bf16[512,256]{1,0:T(8,128)(2,1)S(1)}, u32[]{:S(2)}, u32[]{:S(2)}) collective-permute-start(bf16[512,256]{1,0:T(8,128)(2,1)S(1)} %get-tuple-element.47), channel_id=1, source_target_pairs={{1,47},{2,78},{3,109},{4,140},{5,171},{16,25},{17,56},{18,87},{19,... | collective-permute-start | bytes 786440 | tf_op jit(solution)/shard_map/ppermute | solution.py:290
  34.8 15.3 %conditional.3 = (bf16[512,256]{1,0:T(8,128)(2,1)S(1)}) conditional(s32[]{:T(128)} %convert_element_type.11, (bf16[32,32,256]{2,1,0:T(8,128)(2,1)S(1)}, s32[32,32]{1,0:T(8,128)S(1)}) %tuple.22, () %tuple.23), branch_computations={%region_2.3_spmd, %region_3.4_spmd} | conditional | flops 268435456 | bytes 1835016 | solution.py:287
  34.8 14.8 %all_to_all.31 = bf16[32,32,256]{2,1,0:T(8,128)(2,1)S(1)} all-to-all(bf16[32,32,256]{2,1,0:T(8,128)(2,1)S(1)} %get-tuple-element.22), channel_id=1, replica_groups=mesh['alpha'=32,'beta'=16] {'alpha'}, dimensions={0} | all-to-all | bytes 1048576 | tf_op jit(solution)/shard_map/cond/branch_0_fun/all_to_all | solution.py:264
  49.5 0.6 branch_0_fun.1
  50.1 1.5 %collective-permute-start.1 = (bf16[512,256]{1,0:T(8,128)(2,1)S(1)}, bf16[512,256]{1,0:T(8,128)(2,1)S(1)}, u32[]{:S(2)}, u32[]{:S(2)}) collective-permute-start(bf16[512,256]{1,0:T(8,128)(2,1)S(1)} %get-tuple-element.48), channel_id=1, source_target_pairs={{6,202},{7,233},{8,264},{9,295},{10,326},{11,357},{12,388},{13,419... | collective-permute-start | bytes 786440 | tf_op jit(solution)/shard_map/ppermute | solution.py:291
  51.6 0.8 %shard_map.60 = bf16[512,512]{1,0:T(8,128)(2,1)} custom-call(bf16[512,512]{1,0:T(8,128)(2,1)S(1)} %get-tuple-element.42.from_ref), custom_call_target="tpu_custom_call" | custom-call | bytes 1048576 | tf_op jit(solution)/shard_map/pallas_call | solution.py:194
  52.5 12.5 %all-to-all-start.4 = ((bf16[32,16,512]{2,1,0:T(8,128)(2,1)}), bf16[32,16,512]{2,1,0:T(8,128)(2,1)S(1)}, u32[]{:S(2)}, u32[]{:S(2)}) async-start(bf16[32,16,512]{2,1,0:T(8,128)(2,1)} %bitcast.12), calls=%async_computation.4 | async-start | bytes 1048576 | tf_op jit(solution)/shard_map/all_to_all | solution.py:293
  65.0 0.7 collective-permute-start.2
  65.7 0.2 shard_map.59
  66.0 13.7 %all-to-all-done.4 = bf16[32,16,512]{2,1,0:T(8,128)(2,1)S(1)} async-done(((bf16[32,16,512]{2,1,0:T(8,128)(2,1)}), bf16[32,16,512]{2,1,0:T(8,128)(2,1)S(1)}, u32[]{:S(2)}, u32[]{:S(2)}) %all-to-all-start.4) | async-done | bytes 524320 | tf_op jit(solution)/shard_map/all_to_all | solution.py:293
  79.7 1.0 %shard_map.62 = (f32[256,512]{1,0:T(8,128)S(1)}, f32[256,512]{1,0:T(8,128)}) custom-call(bf16[256,512]{1,0:T(8,128)(2,1)S(1)} %get-tuple-element.39.table_ref, bf16[512,512]{1,0:T(8,128)(2,1)S(1)} %bitcast.19, f32[256,512]{1,0:T(8,128)S(1)} %shard_map.61.turned_ref), custom_call_target="tpu_custom_call" | custom-call | flops 30000001024 | bytes 1310720 | tf_op jit(solution)/shard_map/pallas_call | solution.py:194
  (19 shorter events, 0.6 us)
Async XLA Ops:
  1.5 8.1 %copy-start.3 = (bf16[32,32]{1,0:T(8,128)(2,1)S(1)}, bf16[32,32]{1,0:T(8,128)(2,1)}, u32[]{:S(2)}) copy-start(bf16[32,32]{1,0:T(8,128)(2,1)} %param.13) | copy-start | bytes 6148
  1.5 13.9 %all-to-all-start.2 = ((s32[32,1,48]{2,1,0:T(1,128)}), s32[32,1,48]{2,1,0:T(1,128)S(1)}, u32[]{:S(2)}, u32[]{:S(2)}) async-start(s32[32,1,48]{2,1,0:T(1,128)} %bitcast.8), calls=%async_computation.2 | async-start | bytes 32768 | tf_op jit(solution)/shard_map/all_to_all | solution.py:224
  9.8 0.8 copy-start.1
  10.6 0.8 copy-start.2
  10.7 4.7 %copy-start = (bf16[256,512]{1,0:T(8,128)(2,1)S(1)}, bf16[256,512]{1,0:T(8,128)(2,1)}, u32[]{:S(2)}) copy-start(bf16[256,512]{1,0:T(8,128)(2,1)} %coeffs_ref.1) | copy-start | bytes 786436
  16.6 16.1 %all-to-all-start.3 = ((bf16[32,16,512]{2,1,0:T(8,128)(2,1)}), bf16[32,16,512]{2,1,0:T(8,128)(2,1)S(1)}, u32[]{:S(2)}, u32[]{:S(2)}) async-start(bf16[32,16,512]{2,1,0:T(8,128)(2,1)} %bitcast.10), calls=%async_computation.3 | async-start | bytes 1048576 | tf_op jit(solution)/shard_map/all_to_all | solution.py:251
  33.5 32.2 %collective-permute-start = (bf16[512,256]{1,0:T(8,128)(2,1)S(1)}, bf16[512,256]{1,0:T(8,128)(2,1)S(1)}, u32[]{:S(2)}, u32[]{:S(2)}) collective-permute-start(bf16[512,256]{1,0:T(8,128)(2,1)S(1)} %get-tuple-element.47), channel_id=1, source_target_pairs={{1,47},{2,78},{3,109},{4,140},{5,171},{16,25},{17,56},{18,87},{19,... | collective-permute-start | bytes 786440 | tf_op jit(solution)/shard_map/ppermute | solution.py:290
  50.1 15.8 %collective-permute-start.1 = (bf16[512,256]{1,0:T(8,128)(2,1)S(1)}, bf16[512,256]{1,0:T(8,128)(2,1)S(1)}, u32[]{:S(2)}, u32[]{:S(2)}) collective-permute-start(bf16[512,256]{1,0:T(8,128)(2,1)S(1)} %get-tuple-element.48), channel_id=1, source_target_pairs={{6,202},{7,233},{8,264},{9,295},{10,326},{11,357},{12,388},{13,419... | collective-permute-start | bytes 786440 | tf_op jit(solution)/shard_map/ppermute | solution.py:291
  52.5 27.2 %all-to-all-start.4 = ((bf16[32,16,512]{2,1,0:T(8,128)(2,1)}), bf16[32,16,512]{2,1,0:T(8,128)(2,1)S(1)}, u32[]{:S(2)}, u32[]{:S(2)}) async-start(bf16[32,16,512]{2,1,0:T(8,128)(2,1)} %bitcast.12), calls=%async_computation.4 | async-start | bytes 1048576 | tf_op jit(solution)/shard_map/all_to_all | solution.py:293
  65.0 15.7 %collective-permute-start.2 = (bf16[512,256]{1,0:T(8,128)(2,1)S(1)}, bf16[512,256]{1,0:T(8,128)(2,1)S(1)}, u32[]{:S(2)}, u32[]{:S(2)}) collective-permute-start(bf16[512,256]{1,0:T(8,128)(2,1)S(1)} %get-tuple-element.47), channel_id=1, source_target_pairs={{0,0},{20,149},{21,180},{32,1},{33,32},{53,181},{64,2},{65,33},{66... | collective-permute-start | bytes 786440 | tf_op jit(solution)/shard_map/ppermute | solution.py:289

commit v6 on v5

--- a/solution.py
+++ b/solution.py
@@ -35,8 +35,9 @@
     return 3 * chips // 8
 
 
-def ask_kernel(from_ref, ask_ref, wanted_ref):
-    pltpu.sync_copy(from_ref, wanted_ref)
+def ask_kernel(from_ref, ask_ref, wanted_ref, sem):
+    copy = pltpu.make_async_copy(from_ref, wanted_ref, sem)
+    copy.start()
     cap, peers = wanted_ref.shape
     chips = peers // 2
     plane = lax.axis_index("beta")
@@ -45,9 +46,10 @@
     chip = site // 2 - plane - (site % 2) * (chips // 2 - 1)
     chip = jnp.where(chip < 0, chip + chips, chip)
     chip = jnp.where(chip < 0, chip + chips, chip)
+    picks = [(tile == source).astype(F32).astype(BF16) for source in (site, 2 * chip, 2 * chip + 1)]
+    copy.wait()
     wanted = wanted_ref[...].astype(F32).astype(BF16)
-    for part, source in enumerate((site, 2 * chip, 2 * chip + 1)):
-        pick = (tile == source).astype(F32).astype(BF16)
+    for part, pick in enumerate(picks):
         lists = lax.dot_general(pick, wanted, (((1,), (1,)), ((), ())), preferred_element_type=F32)
         ask_ref[:, part * cap : (part + 1) * cap] = lists.astype(jnp.int32)
 
@@ -218,7 +220,7 @@
         (pltpu.with_memory_space_constraint(wanted.T, pltpu.HBM),),
         6 * peers * peers * cap,
         16 * peers * cap,
-        scratch=[VMEM((cap, peers), jnp.int32)],
+        scratch=[VMEM((cap, peers), jnp.int32), pltpu.SemaphoreType.DMA(())],
         spaces=[pltpu.HBM],
     )
     asked = lax.all_to_all(ask, "alpha", split_axis=0, concat_axis=0, tiled=True)

time: 81.3 us -> 81.2 us (level)
  no operation moved by 1% of the time
where the time goes in v6:
time: 81.2 us; the launch traced here: 80.6 us
  starting transfers between devices  29.2 us (36%)
  waiting for transfers between devices  21.6 us (27%)
  blocking collectives  14.8 us (18%)
  Pallas kernels  12.8 us (16%)
  local copies, waits for them, and re-layouts  1.88 us (2%)
    all_to_all x1, blocking collectives, site_sums(): lax.all_to_all(to_sites, 'alpha', split_axis=0, concat_axis=0, tiled=True)  14.8 us
    all_to_all x1, waiting for transfers between devices, local(): lax.all_to_all(to_owners.reshape(peers, cap, cols), 'alpha', split_axis=0...  13.7 us
    pallas_call x10, Pallas kernels, call(): pl.pallas_call(kernel, out_shape=outs, in_specs=[pl.BlockSpec(memory_spac...  12.8 us
    all_to_all x1, starting transfers between devices, local(): lax.all_to_all(to_owners.reshape(peers, cap, cols), 'alpha', split_axis=0...  12.5 us
    all_to_all x1, starting transfers between devices, local(): lax.all_to_all(ask, 'alpha', split_axis=0, concat_axis=0, tiled=True)  7.94 us
    all_to_all x1, starting transfers between devices, local(): lax.all_to_all(found.reshape(peers, cap, cols), 'alpha', split_axis=0, co...  5.29 us
    all_to_all x1, waiting for transfers between devices, local(): lax.all_to_all(found.reshape(peers, cap, cols), 'alpha', split_axis=0, co...  4.05 us
    all_to_all x1, waiting for transfers between devices, local(): lax.all_to_all(ask, 'alpha', split_axis=0, concat_axis=0, tiled=True)  3.83 us
  transfers between devices with their start and end apart: 6, of which 3 were waited for; matrix products, arithmetic and copies ran while one was open for 1% of the time, Pallas kernels for 12%

profile of v6, /device:TPU:195, one launch (start us, length us, event | category | flops | bytes accessed | tf_op | source)
XLA Modules:
  0.0 80.6 jit_solution(2439677767602540846)
XLA Ops:
  0.0 1.5 %shard_map.56 = s32[32,48]{1,0:T(8,128)} custom-call(s32[16,32]{1,0:T(8,128)} %bitcast.28), custom_call_target="tpu_custom_call" | custom-call | flops 98304 | bytes 8192 | tf_op jit(solution)/shard_map/pallas_call | solution.py:196
  1.5 7.9 %all-to-all-start.2 = ((s32[32,1,48]{2,1,0:T(1,128)}), s32[32,1,48]{2,1,0:T(1,128)S(1)}, u32[]{:S(2)}, u32[]{:S(2)}) async-start(s32[32,1,48]{2,1,0:T(1,128)} %bitcast.8), calls=%async_computation.2 | async-start | bytes 32768 | tf_op jit(solution)/shard_map/all_to_all | solution.py:226
  9.6 0.1 broadcast_multiply_fusion
  9.7 0.4 mul.27.kron_ref
  10.1 0.4 copy-done.1
  10.6 0.1 reshape.40.slot_ref
  10.7 0.5 copy-done.2
  11.4 3.8 %all-to-all-done.2 = s32[32,1,48]{2,1,0:T(1,128)S(1)} async-done(((s32[32,1,48]{2,1,0:T(1,128)}), s32[32,1,48]{2,1,0:T(1,128)S(1)}, u32[]{:S(2)}, u32[]{:S(2)}) %all-to-all-start.2) | async-done | bytes 6176 | tf_op jit(solution)/shard_map/all_to_all | solution.py:226
  15.3 1.2 %shard_map.57 = bf16[512,512]{1,0:T(8,128)(2,1)} custom-call(s32[32,16]{1,0:T(8,128)S(1)} %bitcast.23, bf16[256,512]{1,0:T(8,128)(2,1)S(1)} %copy-done), custom_call_target="tpu_custom_call" | custom-call | flops 134217728 | bytes 786432 | tf_op jit(solution)/shard_map/pallas_call | solution.py:196
  16.5 5.3 %all-to-all-start.3 = ((bf16[32,16,512]{2,1,0:T(8,128)(2,1)}), bf16[32,16,512]{2,1,0:T(8,128)(2,1)S(1)}, u32[]{:S(2)}, u32[]{:S(2)}) async-start(bf16[32,16,512]{2,1,0:T(8,128)(2,1)} %bitcast.10), calls=%async_computation.3 | async-start | bytes 1048576 | tf_op jit(solution)/shard_map/all_to_all | solution.py:253
  21.8 6.7 %shard_map.55 = (bf16[512,512]{1,0:T(8,128)(2,1)S(1)}, bf16[512,512]{1,0:T(8,128)(2,1)S(1)}) custom-call(s32[8,1024]{1,0:T(8,128)S(1)} %reshape.40.slot_ref, s32[8,1024]{1,0:T(8,128)S(1)} %reshape.41.sign_ref, bf16[256,256]{1,0:T(8,128)(2,1)S(1)} %mul.27.kron_ref), custom_call_target="tpu_custom_call" | custom-call | flops 6442450944 | bytes 1048576 | tf_op jit(solution)/shard_map/pallas_call | solution.py:196
  28.5 4.1 %all-to-all-done.3 = bf16[32,16,512]{2,1,0:T(8,128)(2,1)S(1)} async-done(((bf16[32,16,512]{2,1,0:T(8,128)(2,1)}), bf16[32,16,512]{2,1,0:T(8,128)(2,1)S(1)}, u32[]{:S(2)}, u32[]{:S(2)}) %all-to-all-start.3) | async-done | bytes 524320 | tf_op jit(solution)/shard_map/all_to_all | solution.py:253
  32.6 0.7 shard_map.58
  33.4 1.3 %collective-permute-start = (bf16[512,256]{1,0:T(8,128)(2,1)S(1)}, bf16[512,256]{1,0:T(8,128)(2,1)S(1)}, u32[]{:S(2)}, u32[]{:S(2)}) collective-permute-start(bf16[512,256]{1,0:T(8,128)(2,1)S(1)} %get-tuple-element.47), channel_id=1, source_target_pairs={{1,47},{2,78},{3,109},{4,140},{5,171},{16,25},{17,56},{18,87},{19,... | collective-permute-start | bytes 786440 | tf_op jit(solution)/shard_map/ppermute | solution.py:292
  34.7 15.3 %conditional.3 = (bf16[512,256]{1,0:T(8,128)(2,1)S(1)}) conditional(s32[]{:T(128)} %convert_element_type.11, (bf16[32,32,256]{2,1,0:T(8,128)(2,1)S(1)}, s32[32,32]{1,0:T(8,128)S(1)}) %tuple.22, () %tuple.23), branch_computations={%region_2.3_spmd, %region_3.4_spmd} | conditional | flops 268435456 | bytes 1835016 | solution.py:289
  34.7 14.8 %all_to_all.31 = bf16[32,32,256]{2,1,0:T(8,128)(2,1)S(1)} all-to-all(bf16[32,32,256]{2,1,0:T(8,128)(2,1)S(1)} %get-tuple-element.22), channel_id=1, replica_groups=mesh['alpha'=32,'beta'=16] {'alpha'}, dimensions={0} | all-to-all | bytes 1048576 | tf_op jit(solution)/shard_map/cond/branch_0_fun/all_to_all | solution.py:266
  49.4 0.6 branch_0_fun.1
  50.0 1.5 %collective-permute-start.1 = (bf16[512,256]{1,0:T(8,128)(2,1)S(1)}, bf16[512,256]{1,0:T(8,128)(2,1)S(1)}, u32[]{:S(2)}, u32[]{:S(2)}) collective-permute-start(bf16[512,256]{1,0:T(8,128)(2,1)S(1)} %get-tuple-element.48), channel_id=1, source_target_pairs={{6,202},{7,233},{8,264},{9,295},{10,326},{11,357},{12,388},{13,419... | collective-permute-start | bytes 786440 | tf_op jit(solution)/shard_map/ppermute | solution.py:293
  51.5 0.8 %shard_map.60 = bf16[512,512]{1,0:T(8,128)(2,1)} custom-call(bf16[512,512]{1,0:T(8,128)(2,1)S(1)} %get-tuple-element.42.from_ref), custom_call_target="tpu_custom_call" | custom-call | bytes 1048576 | tf_op jit(solution)/shard_map/pallas_call | solution.py:196
  52.4 12.5 %all-to-all-start.4 = ((bf16[32,16,512]{2,1,0:T(8,128)(2,1)}), bf16[32,16,512]{2,1,0:T(8,128)(2,1)S(1)}, u32[]{:S(2)}, u32[]{:S(2)}) async-start(bf16[32,16,512]{2,1,0:T(8,128)(2,1)} %bitcast.12), calls=%async_computation.4 | async-start | bytes 1048576 | tf_op jit(solution)/shard_map/all_to_all | solution.py:295
  64.9 0.7 collective-permute-start.2
  65.6 0.2 shard_map.59
  65.9 13.7 %all-to-all-done.4 = bf16[32,16,512]{2,1,0:T(8,128)(2,1)S(1)} async-done(((bf16[32,16,512]{2,1,0:T(8,128)(2,1)}), bf16[32,16,512]{2,1,0:T(8,128)(2,1)S(1)}, u32[]{:S(2)}, u32[]{:S(2)}) %all-to-all-start.4) | async-done | bytes 524320 | tf_op jit(solution)/shard_map/all_to_all | solution.py:295
  79.5 1.0 %shard_map.62 = (f32[256,512]{1,0:T(8,128)S(1)}, f32[256,512]{1,0:T(8,128)}) custom-call(bf16[256,512]{1,0:T(8,128)(2,1)S(1)} %get-tuple-element.39.table_ref, bf16[512,512]{1,0:T(8,128)(2,1)S(1)} %bitcast.19, f32[256,512]{1,0:T(8,128)S(1)} %shard_map.61.turned_ref), custom_call_target="tpu_custom_call" | custom-call | flops 30000001024 | bytes 1310720 | tf_op jit(solution)/shard_map/pallas_call | solution.py:196
  (19 shorter events, 0.6 us)
Async XLA Ops:
  1.5 8.0 %copy-start.3 = (bf16[32,32]{1,0:T(8,128)(2,1)S(1)}, bf16[32,32]{1,0:T(8,128)(2,1)}, u32[]{:S(2)}) copy-start(bf16[32,32]{1,0:T(8,128)(2,1)} %param.13) | copy-start | bytes 6148
  1.5 13.7 %all-to-all-start.2 = ((s32[32,1,48]{2,1,0:T(1,128)}), s32[32,1,48]{2,1,0:T(1,128)S(1)}, u32[]{:S(2)}, u32[]{:S(2)}) async-start(s32[32,1,48]{2,1,0:T(1,128)} %bitcast.8), calls=%async_computation.2 | async-start | bytes 32768 | tf_op jit(solution)/shard_map/all_to_all | solution.py:226
  9.7 0.8 copy-start.1
  10.5 0.8 copy-start.2
  10.6 4.7 %copy-start = (bf16[256,512]{1,0:T(8,128)(2,1)S(1)}, bf16[256,512]{1,0:T(8,128)(2,1)}, u32[]{:S(2)}) copy-start(bf16[256,512]{1,0:T(8,128)(2,1)} %coeffs_ref.1) | copy-start | bytes 786436
  16.5 16.1 %all-to-all-start.3 = ((bf16[32,16,512]{2,1,0:T(8,128)(2,1)}), bf16[32,16,512]{2,1,0:T(8,128)(2,1)S(1)}, u32[]{:S(2)}, u32[]{:S(2)}) async-start(bf16[32,16,512]{2,1,0:T(8,128)(2,1)} %bitcast.10), calls=%async_computation.3 | async-start | bytes 1048576 | tf_op jit(solution)/shard_map/all_to_all | solution.py:253
  33.4 32.2 %collective-permute-start = (bf16[512,256]{1,0:T(8,128)(2,1)S(1)}, bf16[512,256]{1,0:T(8,128)(2,1)S(1)}, u32[]{:S(2)}, u32[]{:S(2)}) collective-permute-start(bf16[512,256]{1,0:T(8,128)(2,1)S(1)} %get-tuple-element.47), channel_id=1, source_target_pairs={{1,47},{2,78},{3,109},{4,140},{5,171},{16,25},{17,56},{18,87},{19,... | collective-permute-start | bytes 786440 | tf_op jit(solution)/shard_map/ppermute | solution.py:292
  50.0 15.8 %collective-permute-start.1 = (bf16[512,256]{1,0:T(8,128)(2,1)S(1)}, bf16[512,256]{1,0:T(8,128)(2,1)S(1)}, u32[]{:S(2)}, u32[]{:S(2)}) collective-permute-start(bf16[512,256]{1,0:T(8,128)(2,1)S(1)} %get-tuple-element.48), channel_id=1, source_target_pairs={{6,202},{7,233},{8,264},{9,295},{10,326},{11,357},{12,388},{13,419... | collective-permute-start | bytes 786440 | tf_op jit(solution)/shard_map/ppermute | solution.py:293
  52.4 27.2 %all-to-all-start.4 = ((bf16[32,16,512]{2,1,0:T(8,128)(2,1)}), bf16[32,16,512]{2,1,0:T(8,128)(2,1)S(1)}, u32[]{:S(2)}, u32[]{:S(2)}) async-start(bf16[32,16,512]{2,1,0:T(8,128)(2,1)} %bitcast.12), calls=%async_computation.4 | async-start | bytes 1048576 | tf_op jit(solution)/shard_map/all_to_all | solution.py:295
  64.9 15.7 %collective-permute-start.2 = (bf16[512,256]{1,0:T(8,128)(2,1)S(1)}, bf16[512,256]{1,0:T(8,128)(2,1)S(1)}, u32[]{:S(2)}, u32[]{:S(2)}) collective-permute-start(bf16[512,256]{1,0:T(8,128)(2,1)S(1)} %get-tuple-element.47), channel_id=1, source_target_pairs={{0,0},{20,149},{21,180},{32,1},{33,32},{53,181},{64,2},{65,33},{66... | collective-permute-start | bytes 786440 | tf_op jit(solution)/shard_map/ppermute | solution.py:291
